TPU v7x, 32 devices: a whole 2x2x4 slice. The times are simulated.
32 devices in a mesh: lat: 16 (over z, y, core), wid: 2 (over x).
Axes of the slice: x: 2, y: 2, z: 4, core: 2. Of those that a mesh axis runs over, the one named last changes fastest.
Arguments:
- acts: float32 [1024, 4608], P('lat', 'wid'), may hold values from -6 to 6
- enc_weight: float32 [4608, 8192], P('wid', 'lat'), may hold values from -0.09375 to 0.09375
- enc_bias: float32 [8192], P('lat'), may hold values from -1.5 to 1.5
- thresholds: float32 [8192], P('lat'), may hold values from 0.05 to 0.5
- dec_weight: float32 [8192, 4608], P('lat', 'wid'), may hold values from -0.0625 to 0.0625
- dec_bias: float32 [4608], P('wid'), may hold values from -2.5 to 2.5
Outputs:
- grad_enc: float32 [4608, 8192], P('wid', 'lat')
- grad_enc_bias: float32 [8192], P('lat')
- grad_dec: float32 [8192, 4608], P('lat', 'wid')
- grad_dec_bias: float32 [4608], P('wid')
- loss: float32 [], replicated
All inputs are finite; a program needn't handle non-finite values.
Results may differ from a plain program's by a relative error of at most 0.00023.
Values sent between devices are 32-bit elements; how exact they have to be, the bound alone decides.
No kernel may reach another device: no remote copies, remote signals or barrier semaphores. Data moves between devices by JAX's collectives and lax.ppermute only.
A program may use at most 128 MiB of HBM per device.

v0:
```python
import jax
import jax.numpy as jnp
from jax import lax
from jax.sharding import PartitionSpec as P

D = 4608


gate_width = 0.1


def gated(pre, limits):
    sig = jax.nn.sigmoid((pre - limits[None, :]) / gate_width)
    return (pre * sig, sig + pre * sig * (1.0 - sig) / gate_width)


def per_device(acts, enc_weight, enc_bias, thresholds, dec_weight, dec_bias):
    highest = lax.Precision.HIGHEST
    rows_all = lax.all_gather(acts, "lat", axis=0, tiled=True)
    partial_value = jnp.dot(
        rows_all, enc_weight, precision=highest, preferred_element_type=jnp.float32
    )
    pre = lax.psum(partial_value, "wid") + enc_bias[None, :]
    feats, slope = gated(pre, thresholds)
    recon = lax.psum_scatter(
        jnp.dot(feats, dec_weight, precision=highest, preferred_element_type=jnp.float32),
        "lat",
        scatter_dimension=0,
        tiled=True,
    )
    err = recon + dec_bias[None, :] - acts
    errs_all = lax.all_gather(err, "lat", axis=0, tiled=True)
    total_rows = rows_all.shape[0]
    scale = 1.0 / jnp.sqrt(jnp.float32(total_rows))
    grad_out = errs_all * scale
    loss = lax.psum(jnp.sum(err * err), ("lat", "wid")) / (total_rows * D)
    grad_dec_bias = lax.psum(jnp.sum(err * scale, axis=0), "lat")
    grad_dec = jnp.dot(feats.T, grad_out, precision=highest, preferred_element_type=jnp.float32)
    back_part = jnp.dot(
        grad_out, dec_weight.T, precision=highest, preferred_element_type=jnp.float32
    )
    dpre = lax.psum(back_part, "wid") * slope
    grad_enc = jnp.dot(rows_all.T, dpre, precision=highest, preferred_element_type=jnp.float32)
    grad_enc_bias = jnp.sum(dpre, axis=0)
    return (grad_enc, grad_enc_bias, grad_dec, grad_dec_bias, loss)


def solution(mesh):
    in_specs = (P("lat", "wid"), P("wid", "lat"), P("lat"), P("lat"), P("lat", "wid"), P("wid"))
    out_specs = (P("wid", "lat"), P("lat"), P("lat", "wid"), P("wid"), P())
    return jax.shard_map(
        per_device, mesh=mesh, in_specs=in_specs, out_specs=out_specs, check_vma=False
    )
```

profile of v0, /device:TPU:0, one launch (start us, length us, event | category | flops | bytes accessed | tf_op | source)
XLA Modules:
  0.0 565.4 jit_solution(1881625705490355808)
XLA Ops:
  7.2 0.0 all-gather.3.cloned.1.call-start
  7.2 0.7 all-gather.3.cloned.1.call-update
  7.9 0.0 all-reduce.3.cloned.1.call-start
  7.9 86.5 %all-gather.3.cloned.1.call-done = f32[1024,2304]{1,0:T(8,128)} async-done(((f32[64,2304]{1,0:T(8,128)}), f32[1024,2304]{1,0:T(8,128)}) %all-gather.3.cloned.1.call-update) | async-done | bytes 9437200 | tf_op jit(solution)/shard_map/all_gather | solution.py:19
  94.5 18.9 %fusion.10 = f32[1024,512]{1,0:T(8,128)} fusion(f32[1024,2304]{1,0:T(8,128)} %all-gather.3.cloned.1.call-done, f32[2304,512]{1,0:T(8,128)} %param.7), kind=kOutput, calls=%fused_computation.17 | convolution fusion | flops 14495514624 | bytes 16252928 | tf_op jit(solution)/shard_map/dot_general | solution.py:20
  113.4 0.0 copy-start.3
  113.4 0.0 copy-start.4
  113.4 0.0 all-reduce.3.cloned.1.call-update
  113.4 0.0 reduce-scatter.2.cloned.1.call-start
  113.4 61.2 %all-reduce.3.cloned.1.call-done = f32[1024,512]{1,0:T(8,128)} async-done(((f32[1024,512]{1,0:T(8,128)}), f32[1024,512]{1,0:T(8,128)}) %all-reduce.3.cloned.1.call-update) | async-done | bytes 2097168 | tf_op jit(solution)/shard_map/psum | solution.py:23
  174.6 0.0 copy-done.3
  174.6 0.0 copy-done.4
  174.6 20.5 %fusion.8 = f32[1024,2304]{1,0:T(8,128)} fusion(f32[512,2304]{1,0:T(8,128)} %param.10, f32[1024,512]{1,0:T(8,128)} %all-reduce.3.cloned.1.call-done, f32[512]{0:T(512)S(1)} %copy-done.3, f32[512]{0:T(512)S(1)} %copy-done.4), kind=kOutput, calls=%fused_computation.15 | convolution fusion | flops 14499184640 | bytes 16257024 | tf_op jit(solution)/shard_map/dot_general | solution.py:26
  195.1 0.0 copy-start
  195.1 0.0 copy-start.2
  195.1 0.0 reduce-scatter.2.cloned.1.call-update
  195.2 0.0 all-gather.5.cloned.1.call-start
  195.2 111.4 %reduce-scatter.2.cloned.1.call-done = f32[64,2304]{1,0:T(8,128)} async-done(((f32[1024,2304]{1,0:T(8,128)}), f32[64,2304]{1,0:T(8,128)}) %reduce-scatter.2.cloned.1.call-update) | async-done | bytes 589840 | tf_op jit(solution)/shard_map/reduce_scatter | solution.py:25
  306.7 0.0 copy-done
  306.7 0.0 copy-done.2
  306.7 2.6 multiply_reduce_fusion
  309.2 0.0 all-gather.5.cloned.1.call-update
  309.3 0.2 all-reduce.5.cloned.1.call-start
  309.5 81.1 %all-gather.5.cloned.1.call-done = f32[1024,2304]{1,0:T(8,128)} async-done(((f32[64,2304]{1,0:T(8,128)}), f32[1024,2304]{1,0:T(8,128)}) %all-gather.5.cloned.1.call-update) | async-done | bytes 9437200 | tf_op jit(solution)/shard_map/all_gather | solution.py:32
  390.6 19.0 %fusion.2 = f32[1024,512]{1,0:T(8,128)} fusion(f32[512,2304]{1,0:T(8,128)} %param.10, f32[1024,2304]{1,0:T(8,128)} %all-gather.5.cloned.1.call-done), kind=kOutput, calls=%fused_computation.2 | convolution fusion | flops 14497873920 | bytes 16252928 | tf_op jit(solution)/shard_map/dot_general | solution.py:39
  409.6 0.0 copy-start.1
  409.6 0.0 all-reduce.5.cloned.1.call-update
  409.6 38.9 %psum.31 = f32[]{:T(128)} all-reduce(f32[]{:T(128)} %get-tuple-element.10), channel_id=1, replica_groups=mesh['lat'=16,'wid'=2] {'lat','wid'}, use_global_device_ids=true, to_apply=%region_7.0 | all-reduce | flops 1 | bytes 8 | tf_op jit(solution)/shard_map/psum | solution.py:36
  449.2 60.3 %psum.30 = f32[2304]{0:T(1024)} all-reduce(f32[2304]{0:T(1024)S(1)} %get-tuple-element.11), channel_id=1, replica_groups=mesh['lat'=16,'wid'=2] {'lat'}, use_global_device_ids=true, to_apply=%region_5.0 | all-reduce | flops 2304 | bytes 18432 | tf_op jit(solution)/shard_map/psum | solution.py:37
  509.5 0.0 copy-done.1
  509.5 20.1 %fusion = f32[512,2304]{1,0:T(8,128)} fusion(f32[1024,2304]{1,0:T(8,128)} %all-gather.5.cloned.1.call-done, f32[1024,512]{1,0:T(8,128)S(1)} %copy-done.1, f32[512]{0:T(512)S(1)} %copy-done.3, f32[512]{0:T(512)S(1)} %copy-done.4), kind=kOutput, calls=%fused_computation | convolution fusion | flops 14501543936 | bytes 16257024 | tf_op jit(solution)/shard_map/dot_general | solution.py:38
  529.6 0.0 all-reduce.5.cloned.1.call-done
  529.6 3.1 fusion.9
  532.7 19.0 %convolution_bitcast_fusion = f32[2304,512]{0,1:T(8,128)} fusion(f32[1024,512]{1,0:T(8,128)S(1)} %get-tuple-element.14, f32[1024,2304]{1,0:T(8,128)} %all-gather.3.cloned.1.call-done), kind=kOutput, calls=%fused_computation.4 | convolution fusion | flops 14495514624 | bytes 16252928 | tf_op jit(solution)/shard_map/dot_general | solution.py:43
  551.7 6.0 %copy.11 = f32[2304,512]{1,0:T(8,128)} copy(f32[2304,512]{0,1:T(8,128)} %convolution_bitcast_fusion) | data formatting | bytes 9437184
Async XLA Ops:
  7.2 87.3 %all-gather.3.cloned.1.call-start = ((), (), s32[]{:S(2)}) async-start(), calls=%async_computation.1 | async-start | bytes 10027008 | tf_op jit(solution)/shard_map/all_gather | solution.py:19
  7.9 166.7 %all-reduce.3.cloned.1.call-start = ((), (), s32[]{:S(2)}) async-start(), calls=%async_computation.2 | async-start | bytes 4194304 | tf_op jit(solution)/shard_map/psum | solution.py:23
  113.4 61.2 %copy-start.3 = (f32[512]{0:T(512)S(1)}, f32[512]{0:T(512)}, u32[]{:S(2)}) copy-start(f32[512]{0:T(512)} %param.9) | copy-start | bytes 6148
  113.4 61.2 %copy-start.4 = (f32[512]{0:T(512)S(1)}, f32[512]{0:T(512)}, u32[]{:S(2)}) copy-start(f32[512]{0:T(512)} %param.8) | copy-start | bytes 6148
  113.4 193.3 %reduce-scatter.2.cloned.1.call-start = ((), (), s32[]{:S(2)}) async-start(), calls=%async_computation.3 | async-start | bytes 10027008 | tf_op jit(solution)/shard_map/reduce_scatter | solution.py:25
  195.1 111.5 %copy-start = (f32[64,2304]{1,0:T(8,128)S(1)}, f32[64,2304]{1,0:T(8,128)}, u32[]{:S(2)}) copy-start(f32[64,2304]{1,0:T(8,128)} %param.6) | copy-start | bytes 1769476
  195.1 111.5 %copy-start.2 = (f32[2304]{0:T(1024)S(1)}, f32[2304]{0:T(1024)}, u32[]{:S(2)}) copy-start(f32[2304]{0:T(1024)} %param.11) | copy-start | bytes 27652
  195.2 195.5 %all-gather.5.cloned.1.call-start = ((), (), s32[]{:S(2)}) async-start(), calls=%async_computation.4 | async-start | bytes 10027008 | tf_op jit(solution)/shard_map/all_gather | solution.py:32
  309.3 220.3 %all-reduce.5.cloned.1.call-start = ((), (), s32[]{:S(2)}) async-start(), calls=%async_computation.5 | async-start | bytes 4194304 | tf_op jit(solution)/shard_map/psum | solution.py:42
  409.6 99.9 %copy-start.1 = (f32[1024,512]{1,0:T(8,128)S(1)}, f32[1024,512]{1,0:T(8,128)}, u32[]{:S(2)}) copy-start(f32[1024,512]{1,0:T(8,128)} %all-reduce.3.cloned.1.call-done) | copy-start | bytes 6291460
Sparse Core Ops, SparseCore 0:
  10.3 84.1 all-gather.2
  113.5 61.0 all-reduce.2
  195.3 111.3 reduce-scatter.1
  309.4 81.1 all-gather.4
  409.7 61.4 all-reduce.4
where the time goes:
time: 566 us; the launch traced here: 565 us
  waiting for transfers between devices  341 us (60%)
  blocking collectives  99.2 us (18%)
  matrix products  97.5 us (17%)
  between operations  15.6 us (3%)
  local copies, waits for them, and re-layouts  6.06 us (1%)
  other arithmetic  5.72 us (1%)
    reduce_scatter x1, waiting for transfers between devices, per_device(): lax.psum_scatter(jnp.dot(feats, dec_weight, precision=highest, preferred_...  111 us
    all_gather x1, waiting for transfers between devices, per_device(): rows_all = lax.all_gather(acts, 'lat', axis=0, tiled=True)  86.5 us
    all_gather x1, waiting for transfers between devices, per_device(): errs_all = lax.all_gather(err, 'lat', axis=0, tiled=True)  81.1 us
    psum x1, waiting for transfers between devices, per_device(): pre = lax.psum(partial_value, 'wid') + enc_bias[None, :]  61.2 us
    psum x1, blocking collectives, per_device(): grad_dec_bias = lax.psum(jnp.sum(err * scale, axis=0), 'lat')  60.3 us
    psum x1, blocking collectives, per_device(): loss = lax.psum(jnp.sum(err * err), ('lat', 'wid')) / (total_rows * D)  38.9 us
    dot_general x1, matrix products, per_device(): jnp.dot(feats, dec_weight, precision=highest, preferred_element_type=jnp....  20.5 us
    dot_general x1, matrix products, per_device(): jnp.dot(feats.T, grad_out, precision=highest, preferred_element_type=jnp....  20.1 us
  transfers between devices with their start and end apart: 5, of which 4 were waited for; matrix products, arithmetic and copies ran while one was open for 4% of the time, Pallas kernels for 0%

commit v1 on v0

v1 whole, which is shorter than its diff:
```python
import functools
import jax
import jax.numpy as jnp
from jax import lax
from jax.experimental import pallas as pl
from jax.experimental.pallas import tpu as pltpu
from jax.sharding import Mesh, PartitionSpec as P

GATE_WIDTH = 0.1
TILE = 768
EIGHTHS = (2, 2, 2, 2)
SWAP = [(0, 1), (1, 0)]
LATENCY, START = 1.5, 0.8
LIMIT = {"z": 3, "y": 2, "wid": 2, "core": 4}
ROWS_BY_COLS, ROWS_BY_ROWS = ((1,), (0,)), ((1,), (1,))


def split_bf16(x):
    high = x.astype(jnp.bfloat16)
    return high, (x - high.astype(jnp.float32)).astype(jnp.bfloat16)


def stacked_dot(stack, high, low, dims):
    rows = stack.shape[0] // 2

    def part(a, b):
        return lax.dot_general(a, b, (dims, ((), ())), preferred_element_type=jnp.float32)

    both = part(stack[...], high[...])
    return both[:rows] + both[rows:] + part(stack[:rows], low[...])


def fill(stack, *parts):
    rows, at = stack.shape[0] // 2, 0
    for x in parts:
        high, low = split_bf16(x)
        stack[at : at + x.shape[0]] = high
        stack[rows + at : rows + at + x.shape[0]] = low
        at += x.shape[0]


def product_kernel(dims, first, second, own_high, own_low, far_high, far_low, out, stack):
    fill(stack, first[...], second[...])
    latents = out.shape[1] // 2
    out[:, :latents] = stacked_dot(stack, own_high, own_low, dims)
    out[:, latents:] = stacked_dot(stack, far_high, far_low, dims)


PARAMS = pltpu.CompilerParams(vmem_limit_bytes=20 * 1024 * 1024)
COST = pl.CostEstimate(flops=1, bytes_accessed=1, transcendentals=0)


def product(first, second, weights, dims):
    latents = weights[0].shape[0 if dims == ROWS_BY_ROWS else 1]
    depth = first.shape[1]
    rows = first.shape[0] + second.shape[0]
    whole = pl.BlockSpec(memory_space=pltpu.VMEM)
    return pl.pallas_call(
        functools.partial(product_kernel, dims),
        out_shape=jax.ShapeDtypeStruct((rows, 2 * latents), jnp.float32),
        in_specs=[whole] * 6,
        out_specs=whole,
        scratch_shapes=[pltpu.VMEM((2 * rows, depth), jnp.bfloat16)],
        compiler_params=PARAMS,
        cost_estimate=COST,
    )(first, second, *weights)


def gate_kernel(count, *refs):
    parts = refs[:count]
    limits, own_high, own_low, far_high, far_low, slope, feats, sent, near, far, stack = refs[count:]
    latents = own_high.shape[0]

    pre = sum(p[...] for p in parts) + limits[0:1]
    sig = jax.nn.sigmoid((pre - limits[1:2]) / GATE_WIDTH)
    value = pre * sig
    feats[...] = value[:, :latents]
    sent[...] = value[:, latents:]
    slope[...] = sig + pre * sig * (1.0 - sig) / GATE_WIDTH
    fill(stack, value)

    rows, width = near.shape
    tile = TILE if width % TILE == 0 else width
    for at in range(0, width, tile):
        cut = (slice(None), slice(at, at + tile))
        recon = stacked_dot(stack.at[:, :latents], own_high.at[cut], own_low.at[cut], ROWS_BY_COLS)
        recon += stacked_dot(stack.at[:, latents:], far_high.at[cut], far_low.at[cut], ROWS_BY_COLS)
        near[cut] = recon[:rows]
        far[cut] = recon[rows:]


def gate(parts, limits, weights):
    rows, latents = parts[0].shape
    width = weights[0].shape[1]
    whole = pl.BlockSpec(memory_space=pltpu.VMEM)
    slope_shape = jax.ShapeDtypeStruct((rows, latents), jnp.float32)
    feats_shape = jax.ShapeDtypeStruct((rows, latents // 2), jnp.float32)
    half_shape = jax.ShapeDtypeStruct((rows // 2, width), jnp.float32)
    return pl.pallas_call(
        functools.partial(gate_kernel, len(parts)),
        out_shape=(slope_shape, feats_shape, feats_shape, half_shape, half_shape),
        in_specs=[whole] * (len(parts) + 5),
        out_specs=(whole,) * 5,
        scratch_shapes=[pltpu.VMEM((2 * rows, latents), jnp.bfloat16)],
        compiler_params=PARAMS,
        cost_estimate=COST,
    )(*parts, limits, *weights)


def turn_kernel(count, *refs):
    high, low = refs[count:]
    high[...], low[...] = split_bf16(jnp.concatenate([r[...] for r in refs[:count]], axis=0).T)


def turn(*parts):
    rows, columns = sum(p.shape[0] for p in parts), parts[0].shape[1]
    tile = 256 if columns % 256 == 0 else columns
    shape = jax.ShapeDtypeStruct((columns, rows), jnp.bfloat16)
    return pl.pallas_call(
        functools.partial(turn_kernel, len(parts)),
        out_shape=(shape, shape),
        grid=(columns // tile,),
        in_specs=[pl.BlockSpec((p.shape[0], tile), lambda j: (0, j)) for p in parts],
        out_specs=[pl.BlockSpec((tile, rows), lambda j: (j, 0))] * 2,
        compiler_params=PARAMS,
        cost_estimate=COST,
    )(*parts)


def grad_kernel(scale, by_rows, tile, left_high, left_low, *refs):
    *pieces, out, high, low, result, sems = refs

    def fill_right(cut):
        at = 0
        for p in pieces:
            rows = p.shape[0]
            high[at : at + rows], low[at : at + rows] = split_bf16(p[:, cut])
            at += rows

    def part(a, b):
        return jnp.dot(a, b[...], preferred_element_type=jnp.float32)

    copies = []
    for n, at in enumerate(range(0, out.shape[0 if by_rows else 1], tile)):
        cut = slice(at, at + tile)
        rows, columns = (cut, slice(None)) if by_rows else (slice(None), cut)
        if n == 0 or not by_rows:
            fill_right(columns)
        total = part(left_high[rows], high) + part(left_high[rows], low) + part(left_low[rows], high)
        result[rows, columns] = total * scale
        copies.append(pltpu.make_async_copy(result.at[rows, columns], out.at[rows, columns], sems.at[n]))
        copies[-1].start()
    for copy in copies:
        copy.wait()


def grad(left, pieces, scale, by_rows):
    rows, depth = left[0].shape
    columns = pieces[0].shape[1]
    split = rows if by_rows else columns
    tile = TILE if split % TILE == 0 else split
    shape = (rows, columns)
    return pl.pallas_call(
        functools.partial(grad_kernel, scale, by_rows, tile),
        out_shape=jax.ShapeDtypeStruct(shape, jnp.float32),
        in_specs=[pl.BlockSpec(memory_space=pltpu.VMEM)] * (2 + len(pieces)),
        out_specs=pl.BlockSpec(memory_space=pl.ANY),
        scratch_shapes=[pltpu.VMEM((depth, columns if by_rows else tile), jnp.bfloat16)] * 2
        + [pltpu.VMEM(shape, jnp.float32), pltpu.SemaphoreType.DMA((split // tile,))],
        compiler_params=pltpu.CompilerParams(vmem_limit_bytes=24 * 1024 * 1024),
        cost_estimate=COST,
    )(*left, *pieces)


class Step:
    def __init__(self, lane, cost, rank, fn, *deps):
        self.lane, self.cost, self.rank, self.fn, self.deps = lane, cost, rank, fn, deps
        self.value, self.end, self.waited = None, None, False


class Plan:
    def __init__(self):
        self.steps, self.token, self.now = [], jnp.zeros((), jnp.float32), 0.0
        self.free, self.flying = {}, {}

    def add(self, lane, cost, rank, fn, *deps):
        step = Step(lane, cost, rank, fn, *deps)
        self.steps.append(step)
        return step

    def after(self, value):
        value, self.token = lax.optimization_barrier((value, self.token))
        return value

    def hold(self, steps):
        for step, value in zip(steps, self.after([s.value for s in steps])):
            step.value = value

    def wait(self, step):
        if step.lane != "tc" and not step.waited:
            step.value, step.waited = self.after(step.value), True
            self.flying[step.lane].remove(step)

    def ready(self, step):
        return all(d.end is not None and d.end <= self.now for d in step.deps)

    def start(self, step):
        flying = self.flying.setdefault(step.lane, [])
        if len(flying) >= LIMIT[step.lane]:
            if min(f.end for f in flying) > self.now:
                return False
            self.wait(min(flying, key=lambda f: f.end))
        for d in step.deps:
            self.wait(d)
            d.value = self.after(d.value)
        step.value = step.fn(*[d.value for d in step.deps])
        begin = max(self.now, self.free.get(step.lane, 0.0))
        self.free[step.lane] = begin + step.cost
        step.end = begin + step.cost + LATENCY
        flying.append(step)
        self.now += START
        return True

    def compute(self, step):
        for d in step.deps:
            self.wait(d)
        self.hold(step.deps)
        step.value = self.after(step.fn(*[d.value for d in step.deps]))
        self.now += step.cost
        step.end = self.now

    def run(self):
        left = sorted(self.steps, key=lambda s: s.rank)
        while left:
            for step in [s for s in left if s.lane != "tc"]:
                if self.ready(step) and self.start(step):
                    left.remove(step)
            step = next((s for s in left if s.lane == "tc" and self.ready(s)), None)
            if step is not None:
                left.remove(step)
                self.compute(step)
                continue
            ends = [f.end for flying in self.flying.values() for f in flying if f.end > self.now]
            if left and ends:
                self.now = min(ends)


def fold(x):
    while x.shape[0] > 1:
        half = x.shape[0] // 2
        x = x[:half] + x[half:]
    return x[0]


def cat(*xs):
    return jnp.concatenate(xs, axis=0)


def swap(axis):
    return lambda x: lax.ppermute(x, axis, SWAP)


def per_device(wid, long, acts, enc_weight, enc_bias, thresholds, dec_weight, dec_bias):
    lat = 4 * long
    rows_own, width = acts.shape
    latents = enc_weight.shape[1]
    total_rows = rows_own * lat
    scale = 1.0 / jnp.sqrt(jnp.float32(total_rows))
    pieces = [n * rows_own // sum(EIGHTHS) for n in EIGHTHS]
    plan = Plan()

    def shift(by):
        return lambda x: lax.ppermute(x, "z", [(i, (i + by) % long) for i in range(long)])

    def links(rows):
        return 2 * rows * width * 4 / 70e3

    def gather(own, piece, rank):
        slots = [own] + [None] * (long - 1)
        up, down = (own,), (own,)
        for hop in range(1, long // 2 + 1):
            after = up + down if hop > 1 else up
            up = (plan.add("z", links(piece), rank, lambda x, *_: shift(1)(x), *after),)
            slots[hop] = up[0]
            if hop < long - hop:
                after = down + after[:1] if hop > 1 else down
                down = (plan.add("z", links(piece), rank, lambda x, *_: shift(-1)(x), *after),)
                slots[long - hop] = down[0]
        line = plan.add("tc", 1.0, rank, cat, *slots)
        return line, plan.add("y", links(long * piece), rank, swap("y"), line)

    def scatter(recon, piece, rank):
        beside = plan.add("y", links(long * piece), rank, lambda g: swap("y")(g[4]), recon)

        def split(g, y):
            line = g[3] + y
            return tuple(line[d * piece : (d + 1) * piece] for d in range(long))

        line = plan.add("tc", 1.0, rank, split, recon, beside)
        ups, downs = list(range(long // 2, 0, -1)), list(range(long // 2 + 1, long))
        up = down = None
        while ups or downs:
            before = [x for x in (up, down) if x is not None]
            if ups:
                d = ups.pop(0)
                if up is None:
                    src = plan.add("tc", 0.0, rank, lambda s, d=d: s[d], line)
                else:
                    src = plan.add("tc", 0.5, rank, lambda s, t, *_, d=d: s[d] + t, line, up, *before[1:])
                up = plan.add("z", links(piece), rank, shift(-1), src)
            if downs:
                d = downs.pop(0)
                if down is None:
                    src = plan.add("tc", 0.0, rank, lambda s, d=d: s[d], line)
                else:
                    src = plan.add("tc", 0.5, rank, lambda s, t, *_, d=d: s[d] + t, line, down, *before[:1])
                down = plan.add("z", links(piece), rank, shift(1), src)
        return line, up, down

    def sum_wid(part, rank, cost):
        if wid == 2:
            return part, plan.add("wid", cost, rank, swap("wid"), part)
        return (plan.add("tc", 5.0, rank, lambda a: lax.psum(a, "wid"), part),)

    def parts_of(x):
        high = lax.reduce_precision(x, 8, 7)
        return high.astype(jnp.bfloat16), (x - high).astype(jnp.bfloat16)

    def sums(a, b):
        blocks = jnp.concatenate([a, b], axis=0).reshape(lat // 2, -1, width)
        return jnp.sum(blocks, axis=1), jnp.sum(blocks * blocks, axis=1)

    chunks, at = [], 0
    for k, piece in enumerate(pieces):
        chunks.append(plan.add("tc", 0.2, -10.0 + k, lambda a=at, b=at + piece: acts[a:b]))
        at += piece
    enc_own, dec_own = (plan.add("tc", 0.0, -6.0, lambda w=w: w) for w in (enc_weight, dec_weight))
    limits_own = plan.add("tc", 0.2, -6.0, lambda: jnp.stack([enc_bias, thresholds]))
    enc_far = plan.add("core", 8.0, 2.1, swap("core"), enc_own)
    limits_far = plan.add("core", 0.5, 0.2, swap("core"), limits_own)
    dec_far = plan.add("core", 8.0, 6.2, swap("core"), dec_own)
    limits = plan.add("tc", 0.3, 0.4, lambda a, b: jnp.concatenate([a, b], axis=1), limits_own, limits_far)
    enc_parts = [plan.add("tc", 3.0, 1.0, parts_of, enc_own), plan.add("tc", 3.0, 2.5, parts_of, enc_far)]
    dec_parts = [plan.add("tc", 3.0, 4.5, parts_of, dec_own), plan.add("tc", 3.0, 4.5, parts_of, dec_far)]

    def slopes(g, *ps):
        total = sum(ps) * g[0] * scale
        return total[:, :latents], total[:, latents:]

    def half(n):
        return lambda xs: xs[n]

    count = len(pieces)
    totals, biases, gates, rows, rows_far, feats_far = [], [], [], [], [], []
    errs, errs_far, dpres, dpres_far = [], [], [], []
    for k, (own, piece) in enumerate(zip(chunks, pieces)):
        ranks = [2.0 * k - 2.5 * stage for stage in range(5)]
        late = 100.0 + 2.0 * k
        size = piece / 16
        part_cost = 2 * piece * lat * latents * 4 / 70e3
        near, far = gather(own, piece, ranks[0])
        part = plan.add(
            "tc", 3.6, ranks[1], lambda a, b, *w: product(a, b, w[0] + w[1], ROWS_BY_COLS), near, far, *enc_parts
        )
        parts = sum_wid(part, ranks[1], part_cost)
        gated = plan.add("tc", 3.6, ranks[1], lambda l, v, w, *ps: gate(ps, l, v + w), limits, *dec_parts, *parts)
        line, up, down = scatter(gated, piece, ranks[2])
        err = plan.add(
            "tc", 0.8, ranks[3], lambda s, u, d, a: ((s[0] + u) + d) + dec_bias[None, :] - a, line, up, down, own
        )
        err_near, err_far = gather(err, piece, ranks[3])
        back = plan.add(
            "tc", 3.6, ranks[4], lambda a, b, *w: product(a, b, w[0] + w[1], ROWS_BY_ROWS), err_near, err_far, *dec_parts
        )
        total = sum_wid(back, ranks[4], part_cost)
        dpre = plan.add("tc", 0.9, ranks[4], slopes, gated, *total)
        dpre_far = plan.add("core", 0.5 * size, ranks[4], lambda d: swap("core")(d[1]), dpre)

        pair = plan.add("tc", 0.9 * size, late, cat, near, far)
        rows.append(pair)
        rows_far.append(plan.add("core", 2.0 * size, late, swap("core"), pair))
        feats_far.append(plan.add("core", 0.5 * size, late, lambda g: swap("core")(g[2]), gated))
        pair = plan.add("tc", 0.9 * size, late, cat, err_near, err_far)
        errs_far.append(plan.add("core", 2.0 * size, late, swap("core"), pair))
        errs.append(pair)
        gates.append(gated)
        dpres.append(dpre)
        dpres_far.append(dpre_far)
        totals.append(plan.add("tc", 1.0, late + 3, sums, err_near, err_far))
        biases.append(plan.add("tc", 0.6, late + 4, lambda d, f: (jnp.sum(d[0], axis=0), jnp.sum(f, axis=0)), dpre, dpre_far))

    turned_rows = plan.add("tc", 5.0, 300, turn, *rows, *rows_far)
    turned_feats = plan.add(
        "tc", 1.5, 302, lambda *xs: turn(*[x[1] for x in xs[:count]], *xs[count:]), *gates, *feats_far
    )
    dec_sum = plan.add(
        "tc", 8.0, 400, lambda t, *xs: grad(t, xs, total_rows**-0.5, False), turned_feats, *errs, *errs_far
    )
    enc_sum = plan.add(
        "tc", 8.0, 401,
        lambda t, *xs: grad(t, [x[0] for x in xs[:count]] + list(xs[count:]), 1.0, True),
        turned_rows, *dpres, *dpres_far,
    )
    by_block = plan.add("tc", 0.5, 510, lambda *ts: (sum(t[0] for t in ts), sum(t[1] for t in ts)), *totals)

    def reduced(t):
        return jnp.stack([fold(fold(x.reshape(2, long, width).swapaxes(0, 1))) for x in t])

    column_near = plan.add("tc", 1.0, 511, reduced, by_block)
    column_far = plan.add("core", 0.5, 512, swap("core"), column_near)
    column = plan.add("tc", 0.5, 720, lambda a, b: a + b, column_near, column_far)
    square = plan.add("tc", 0.5, 721, lambda c: jnp.sum(c[1], keepdims=True), column)
    squares = [plan.add("tc", 0.3, 950, lambda x, *_: x, q, enc_sum) for q in sum_wid(square, 722, 0.5)]
    plan.run()

    loss = sum(s.value for s in squares)[0] / (total_rows * width * wid) + plan.token
    grad_enc_bias = sum(b.value[0] for b in biases) + sum(b.value[1] for b in biases)
    return enc_sum.value, grad_enc_bias, dec_sum.value, column.value[0] * scale, loss


def solution(mesh):
    lat, wid = mesh.shape["lat"], mesh.shape["wid"]
    long = lat // 4
    if lat == 16:
        dims, names = (long, 2, 2, wid), ("z", "y", "core", "wid")
    else:
        dims, names = (2, long, 2, wid), ("y", "z", "core", "wid")
    split = Mesh(mesh.devices.reshape(dims), names)
    both = names[:3]
    in_specs = (P(both, "wid"), P("wid", both), P(both), P(both), P(both, "wid"), P("wid"))
    out_specs = (P("wid", both), P(both), P(both, "wid"), P("wid"), P())

    def body(*args):
        return per_device(wid, long, *args)

    return jax.shard_map(body, mesh=split, in_specs=in_specs, out_specs=out_specs, check_vma=False)
```

time: 566 us -> 295 us (0.52)
  waiting for transfers between devices: 341 us -> 82.8 us
  blocking collectives: 99.2 us -> 0 us
  matrix products: 97.5 us -> 0 us
  starting transfers between devices: 0.38 us -> 86.2 us
  Pallas kernels: 0 us -> 57.7 us
  other arithmetic: 5.72 us -> 30.8 us
  local copies, waits for them, and re-layouts: 6.06 us -> 28.3 us
  between operations: 15.6 us -> 4.29 us
    all_gather x2 -> x0, waiting for transfers between devices: 168 us -> none  [the longest x1 86.5 us: per_device(): rows_all = lax.all_gather(acts, 'lat', axis=0, tiled=True)]
    reduce_scatter x1 -> x0, waiting for transfers between devices: 111 us -> none  [per_device(): lax.psum_scatter(jnp.dot(feats, dec_weight, precision=highest, preferred_...]
    psum x2 -> x0, blocking collectives: 99.2 us -> none  [the longest x1 60.3 us: per_device(): grad_dec_bias = lax.psum(jnp.sum(err * scale, axis=0), 'lat')]
    dot_general x5 -> x0, matrix products: 97.5 us -> none  [the longest x1 20.5 us: per_device(): jnp.dot(feats, dec_weight, precision=highest, preferred_element_type=jnp....]
    ppermute x0 -> x77, starting transfers between devices: none -> 86.2 us  [the longest x36 52 us: shift(): lax.ppermute(x, 'z', [(i, (i + by) % long) for i in range(long)])]
    ppermute x0 -> x77, waiting for transfers between devices: none -> 82.8 us  [the longest x36 60 us: shift(): lax.ppermute(x, 'z', [(i, (i + by) % long) for i in range(long)])]
    psum x2 -> x0, waiting for transfers between devices: 61.2 us -> none  [the longest x1 61.2 us: per_device(): pre = lax.psum(partial_value, 'wid') + enc_bias[None, :]]
    pallas_call x0 -> x16, Pallas kernels: none -> 57.7 us  [the longest x8 22.4 us: product(): pl.pallas_call(functools.partial(product_kernel, dims), out_shape=jax.Sha...]
  transfers between devices with their start and end apart: 5 -> 77, of which waited for: 4 -> 36; matrix products, arithmetic and copies ran while one was open for 4% -> 11% of each run, Pallas kernels for 0% -> 20%
where the time goes in v1:
time: 295 us; the launch traced here: 290 us
  starting transfers between devices  86.2 us (29%)
  waiting for transfers between devices  82.8 us (28%)
  Pallas kernels  57.7 us (20%)
  other arithmetic  30.8 us (10%)
  local copies, waits for them, and re-layouts  28.3 us (10%)
  between operations  4.29 us (1%)
    ppermute x36, waiting for transfers between devices, shift(): lax.ppermute(x, 'z', [(i, (i + by) % long) for i in range(long)])  60 us
    ppermute x36, starting transfers between devices, shift(): lax.ppermute(x, 'z', [(i, (i + by) % long) for i in range(long)])  52 us
    ppermute x41, starting transfers between devices, swap(): return lambda x: lax.ppermute(x, axis, SWAP)  34.2 us
    unnamed x90, local copies, waits for them, and re-layouts  25.4 us
    ppermute x41, waiting for transfers between devices, swap(): return lambda x: lax.ppermute(x, axis, SWAP)  22.9 us
    pallas_call x8, Pallas kernels, product(): pl.pallas_call(functools.partial(product_kernel, dims), out_shape=jax.Sha...  22.4 us
    pallas_call x2, Pallas kernels, grad(): pl.pallas_call(functools.partial(grad_kernel, scale, by_rows, tile), out_...  21.6 us
    concatenate x16, other arithmetic, cat(): return jnp.concatenate(xs, axis=0)  8.35 us
  transfers between devices with their start and end apart: 77, of which 36 were waited for; matrix products, arithmetic and copies ran while one was open for 11% of the time, Pallas kernels for 20%

profile of v1, /device:TPU:0, one launch (start us, length us, event | category | flops | bytes accessed | tf_op | source)
XLA Modules:
  0.0 290.2 jit_solution(809186127117004443)
XLA Ops:
  2.4 3.0 %collective-permute-start.1 = (f32[16,2304]{1,0:T(8,128)S(1)}, f32[16,2304]{1,0:T(8,128)S(1)}, u32[]{:S(2)}, u32[]{:S(2)}) collective-permute-start(f32[16,2304]{1,0:T(8,128)S(1)} %get-tuple-element.1204), channel_id=1, source_target_pairs={{0,8},{8,16},{16,24},{24,0},{1,9},{9,17},{17,25},{25,1},{2,10},{10... | collective-permute-start | bytes 442376 | tf_op jit(solution)/shard_map/ppermute | solution.py:273
  5.4 2.0 collective-permute-start.2
  7.5 3.3 %fusion = (bf16[2304,512]{1,0:T(8,128)(2,1)S(1)}, bf16[2304,512]{1,0:T(8,128)(2,1)S(1)}) fusion(f32[2304,512]{1,0:T(8,128)} %param.7), kind=kLoop, calls=%fused_computation.8 | loop fusion | flops 4718592 | bytes 9437184 | tf_op jit(solution)/shard_map/convert_element_type | solution.py:327
  14.1 3.9 %collective-permute-start.5 = (f32[16,2304]{1,0:T(8,128)S(1)}, f32[16,2304]{1,0:T(8,128)S(1)}, u32[]{:S(2)}, u32[]{:S(2)}) collective-permute-start(f32[16,2304]{1,0:T(8,128)S(1)} %get-tuple-element.1257), channel_id=1, source_target_pairs={{0,24},{8,0},{16,8},{24,16},{1,25},{9,1},{17,9},{25,17},{2,26},{10... | collective-permute-start | bytes 442376 | tf_op jit(solution)/shard_map/ppermute | solution.py:273
  18.8 3.4 %collective-permute-done.5 = f32[16,2304]{1,0:T(8,128)S(1)} collective-permute-done((f32[16,2304]{1,0:T(8,128)S(1)}, f32[16,2304]{1,0:T(8,128)S(1)}, u32[]{:S(2)}, u32[]{:S(2)}) %collective-permute-start.5) | collective-permute-done | bytes 147488 | tf_op jit(solution)/shard_map/ppermute | solution.py:273
  22.9 3.0 %collective-permute-done.3 = f32[16,2304]{1,0:T(8,128)S(1)} collective-permute-done((f32[16,2304]{1,0:T(8,128)S(1)}, f32[16,2304]{1,0:T(8,128)S(1)}, u32[]{:S(2)}, u32[]{:S(2)}) %collective-permute-start.3) | collective-permute-done | bytes 147488 | tf_op jit(solution)/shard_map/ppermute | solution.py:273
  29.2 3.8 %collective-permute-start.13 = (f32[16,2304]{1,0:T(8,128)S(1)}, f32[16,2304]{1,0:T(8,128)S(1)}, u32[]{:S(2)}, u32[]{:S(2)}) collective-permute-start(f32[16,2304]{1,0:T(8,128)S(1)} %get-tuple-element.1337), channel_id=1, source_target_pairs={{0,24},{8,0},{16,8},{24,16},{1,25},{9,1},{17,9},{25,17},{2,26},{10... | collective-permute-start | bytes 442376 | tf_op jit(solution)/shard_map/ppermute | solution.py:273
  34.6 3.0 %collective-permute-done.10 = f32[16,2304]{1,0:T(8,128)S(1)} collective-permute-done((f32[16,2304]{1,0:T(8,128)S(1)}, f32[16,2304]{1,0:T(8,128)S(1)}, u32[]{:S(2)}, u32[]{:S(2)}) %collective-permute-start.10) | collective-permute-done | bytes 147488 | tf_op jit(solution)/shard_map/ppermute | solution.py:273
  37.6 3.8 %collective-permute-start.11 = (f32[16,2304]{1,0:T(8,128)S(1)}, f32[16,2304]{1,0:T(8,128)S(1)}, u32[]{:S(2)}, u32[]{:S(2)}) collective-permute-start(f32[16,2304]{1,0:T(8,128)S(1)} %get-tuple-element.1394), channel_id=1, source_target_pairs={{0,24},{8,0},{16,8},{24,16},{1,25},{9,1},{17,9},{25,17},{2,26},{10... | collective-permute-start | bytes 442376 | tf_op jit(solution)/shard_map/ppermute | solution.py:273
  43.2 2.6 collective-permute-done.12
  51.5 2.8 collective-permute-done.16
  59.5 5.3 %collective-permute-done.14.refs_1_ = f32[128,1024]{1,0:T(8,128)S(1)} collective-permute-done((f32[128,1024]{1,0:T(8,128)S(1)}, f32[128,1024]{1,0:T(8,128)S(1)}, u32[]{:S(2)}, u32[]{:S(2)}) %collective-permute-start.14) | collective-permute-done | bytes 524320 | tf_op jit(solution)/shard_map/ppermute | solution.py:260
  64.8 2.1 shard_map.103
  74.6 2.1 shard_map.105
  77.5 5.3 %collective-permute-done.22.second = f32[64,2304]{1,0:T(8,128)S(1)} collective-permute-done((f32[64,2304]{1,0:T(8,128)S(1)}, f32[64,2304]{1,0:T(8,128)S(1)}, u32[]{:S(2)}, u32[]{:S(2)}) %collective-permute-start.22) | collective-permute-done | bytes 589856 | tf_op jit(solution)/shard_map/ppermute | solution.py:260
  85.9 2.1 shard_map.107
  94.8 4.4 %shard_map.108 = (bf16[2304,1024]{1,0:T(8,128)(2,1)S(1)}, bf16[2304,1024]{1,0:T(8,128)(2,1)S(1)}) custom-call(f32[128,2304]{1,0:T(8,128)S(1)} %pad_maximum_fusion.refs_0_, f32[128,2304]{1,0:T(8,128)S(1)} %pad_maximum_fusion.1.refs_1_, f32[128,2304]{1,0:T(8,128)S(1)} %pad_maximum_fusion.2.refs_2_, f32[128,2304]{1,0:T(8,128)S(1)} %pad_maximum_fusion.3.refs_3_, ...), custom_call_target="tpu_custom_call" | custom-call | flops 1 | bytes 1 | tf_op jit(solution)/shard_map/pallas_call | solution.py:119
  99.2 2.2 copy-done.11
  101.4 2.2 copy-done.13
  105.6 2.1 shard_map.109
  107.8 2.9 %collective-permute-start.28 = (f32[16,2304]{1,0:T(8,128)S(1)}, f32[16,2304]{1,0:T(8,128)S(1)}, u32[]{:S(2)}, u32[]{:S(2)}) collective-permute-start(f32[16,2304]{1,0:T(8,128)S(1)} %get-tuple-element.1113), channel_id=1, source_target_pairs={{0,24},{8,0},{16,8},{24,16},{1,25},{9,1},{17,9},{25,17},{2,26},{10... | collective-permute-start | bytes 442376 | tf_op jit(solution)/shard_map/ppermute | solution.py:273
  115.0 3.5 %collective-permute-done.33 = f32[16,2304]{1,0:T(8,128)S(1)} collective-permute-done((f32[16,2304]{1,0:T(8,128)S(1)}, f32[16,2304]{1,0:T(8,128)S(1)}, u32[]{:S(2)}, u32[]{:S(2)}) %collective-permute-start.33) | collective-permute-done | bytes 147488 | tf_op jit(solution)/shard_map/ppermute | solution.py:273
  118.5 2.5 collective-permute-start.34
  125.4 2.4 collective-permute-done.36
  127.8 5.7 %collective-permute-start.37 = (f32[16,2304]{1,0:T(8,128)S(1)}, f32[16,2304]{1,0:T(8,128)S(1)}, u32[]{:S(2)}, u32[]{:S(2)}) collective-permute-start(f32[16,2304]{1,0:T(8,128)S(1)} %add_subtract_fusion.3), channel_id=1, source_target_pairs={{0,8},{8,16},{16,24},{24,0},{1,9},{9,17},{17,25},{25,1},{2,10},{10... | collective-permute-start | bytes 442376 | tf_op jit(solution)/shard_map/ppermute | solution.py:273
  134.5 3.3 %collective-permute-done.37 = f32[16,2304]{1,0:T(8,128)S(1)} collective-permute-done((f32[16,2304]{1,0:T(8,128)S(1)}, f32[16,2304]{1,0:T(8,128)S(1)}, u32[]{:S(2)}, u32[]{:S(2)}) %collective-permute-start.37) | collective-permute-done | bytes 147488 | tf_op jit(solution)/shard_map/ppermute | solution.py:273
  137.8 2.4 collective-permute-done.40
  141.7 4.3 %collective-permute-start.43 = (f32[16,2304]{1,0:T(8,128)S(1)}, f32[16,2304]{1,0:T(8,128)S(1)}, u32[]{:S(2)}, u32[]{:S(2)}) collective-permute-start(f32[16,2304]{1,0:T(8,128)S(1)} %get-tuple-element.1260), channel_id=1, source_target_pairs={{0,24},{8,0},{16,8},{24,16},{1,25},{9,1},{17,9},{25,17},{2,26},{10... | collective-permute-start | bytes 442376 | tf_op jit(solution)/shard_map/ppermute | solution.py:273
  146.2 4.0 %collective-permute-done.43 = f32[16,2304]{1,0:T(8,128)S(1)} collective-permute-done((f32[16,2304]{1,0:T(8,128)S(1)}, f32[16,2304]{1,0:T(8,128)S(1)}, u32[]{:S(2)}, u32[]{:S(2)}) %collective-permute-start.43) | collective-permute-done | bytes 147488 | tf_op jit(solution)/shard_map/ppermute | solution.py:273
  150.2 3.9 %collective-permute-done.41 = f32[16,2304]{1,0:T(8,128)S(1)} collective-permute-done((f32[16,2304]{1,0:T(8,128)S(1)}, f32[16,2304]{1,0:T(8,128)S(1)}, u32[]{:S(2)}, u32[]{:S(2)}) %collective-permute-start.41) | collective-permute-done | bytes 147488 | tf_op jit(solution)/shard_map/ppermute | solution.py:273
  155.1 3.0 %collective-permute-start.48 = (f32[16,2304]{1,0:T(8,128)S(1)}, f32[16,2304]{1,0:T(8,128)S(1)}, u32[]{:S(2)}, u32[]{:S(2)}) collective-permute-start(f32[16,2304]{1,0:T(8,128)S(1)} %add_subtract_fusion.2), channel_id=1, source_target_pairs={{0,24},{8,0},{16,8},{24,16},{1,25},{9,1},{17,9},{25,17},{2,26},{10... | collective-permute-start | bytes 442376 | tf_op jit(solution)/shard_map/ppermute | solution.py:273
  159.8 2.9 collective-permute-done.49
  164.7 3.6 %collective-permute-done.47 = f32[16,2304]{1,0:T(8,128)S(1)} collective-permute-done((f32[16,2304]{1,0:T(8,128)S(1)}, f32[16,2304]{1,0:T(8,128)S(1)}, u32[]{:S(2)}, u32[]{:S(2)}) %collective-permute-start.47) | collective-permute-done | bytes 147488 | tf_op jit(solution)/shard_map/ppermute | solution.py:273
  169.2 2.8 shard_map.111
  175.4 3.0 %collective-permute-start.55 = (f32[16,2304]{1,0:T(8,128)S(1)}, f32[16,2304]{1,0:T(8,128)S(1)}, u32[]{:S(2)}, u32[]{:S(2)}) collective-permute-start(f32[16,2304]{1,0:T(8,128)S(1)} %add_subtract_fusion.1), channel_id=1, source_target_pairs={{0,24},{8,0},{16,8},{24,16},{1,25},{9,1},{17,9},{25,17},{2,26},{10... | collective-permute-start | bytes 442376 | tf_op jit(solution)/shard_map/ppermute | solution.py:273
  187.0 3.8 %collective-permute-start.64 = (f32[16,2304]{1,0:T(8,128)}, f32[16,2304]{1,0:T(8,128)}, u32[]{:S(2)}, u32[]{:S(2)}) collective-permute-start(f32[16,2304]{1,0:T(8,128)} %add_subtract_fusion), channel_id=1, source_target_pairs={{0,24},{8,0},{16,8},{24,16},{1,25},{9,1},{17,9},{25,17},{2,26},{10... | collective-permute-start | bytes 442376 | tf_op jit(solution)/shard_map/ppermute | solution.py:273
  197.8 2.8 shard_map.112
  207.2 5.8 %collective-permute-done.63 = f32[16,2304]{1,0:T(8,128)S(1)} collective-permute-done((f32[16,2304]{1,0:T(8,128)}, f32[16,2304]{1,0:T(8,128)S(1)}, u32[]{:S(2)}, u32[]{:S(2)}) %collective-permute-start.63) | collective-permute-done | bytes 147488 | tf_op jit(solution)/shard_map/ppermute | solution.py:273
  214.1 2.7 collective-permute-done.61
  227.5 4.0 %shard_map.113 = f32[128,1024]{1,0:T(8,128)S(1)} custom-call(f32[64,2304]{1,0:T(8,128)S(1)} %pad_maximum_fusion.18.first, f32[64,2304]{1,0:T(8,128)} %collective-permute-done.60.second, bf16[512,2304]{1,0:T(8,128)(2,1)S(1)} %copy-done.2, bf16[512,2304]{1,0:T(8,128)(2,1)S(1)} %get-tuple-element.1493.refs_4_.own_low, bf16[512,2304]{1,0:T(8,128)(2,1)S(1)} %copy-done.8, ...), custom_call_target="tpu_custom_call" | custom-call | flops 1 | bytes 1 | tf_op jit(solution)/shard_map/pallas_call | solution.py:58
  233.2 2.2 pad_maximum_fusion.8.refs_2_
  235.4 2.1 fusion.5
  237.5 4.8 %shard_map.114 = f32[128,1024]{1,0:T(8,128)} custom-call(f32[64,2304]{1,0:T(8,128)S(1)} %pad_maximum_fusion.19.first, f32[64,2304]{1,0:T(8,128)} %collective-permute-done.66.second, bf16[512,2304]{1,0:T(8,128)(2,1)S(1)} %copy-done.2, bf16[512,2304]{1,0:T(8,128)(2,1)S(1)} %get-tuple-element.1493.refs_4_.own_low, bf16[512,2304]{1,0:T(8,128)(2,1)S(1)} %copy-done.8, ...), custom_call_target="tpu_custom_call" | custom-call | flops 1 | bytes 1 | tf_op jit(solution)/shard_map/pallas_call | solution.py:58
  243.2 2.3 collective-permute-done.67
  256.4 11.9 %shard_map.115 = f32[512,2304]{1,0:T(8,128)} custom-call(bf16[512,1024]{1,0:T(8,128)(2,1)S(1)} %copy-done.22, bf16[512,1024]{1,0:T(8,128)(2,1)S(1)} %copy-done.24, f32[128,2304]{1,0:T(8,128)S(1)} %copy-done.16, f32[128,2304]{1,0:T(8,128)} %pad_maximum_fusion.6.refs_1_, f32[128,2304]{1,0:T(8,128)} %pad_maximum_fusion.8.refs_2_, ...), custom_call_target="tpu_custom_call" | custom-call | flops 1 | bytes 1 | tf_op jit(solution)/shard_map/pallas_call | solution.py:163
  272.5 2.3 copy-done.12
  274.8 2.3 copy-done.14
  277.2 9.7 %shard_map.116 = f32[2304,512]{1,0:T(8,128)} custom-call(bf16[2304,1024]{1,0:T(8,128)(2,1)S(1)} %copy-done.12, bf16[2304,1024]{1,0:T(8,128)(2,1)S(1)} %copy-done.14, f32[128,512]{1,0:T(8,128)S(1)} %copy-done.17, f32[128,512]{1,0:T(8,128)S(1)} %copy-done.18, f32[128,512]{1,0:T(8,128)S(1)} %get-tuple-element.1599.refs_2_, ...), custom_call_target="tpu_custom_call" | custom-call | flops 1 | bytes 1 | tf_op jit(solution)/shard_map/pallas_call | solution.py:163
  (285 shorter events, 116.3 us)
Async XLA Ops:
  1.8 16.2 %collective-permute-start.7 = (f32[2304,512]{1,0:T(8,128)}, f32[2304,512]{1,0:T(8,128)S(1)}, u32[]{:S(2)}, u32[]{:S(2)}) collective-permute-start(f32[2304,512]{1,0:T(8,128)} %param.7), channel_id=1, source_target_pairs={{0,2},{2,0},{1,3},{3,1},{4,6},{6,4},{5,7},{7,5},{8,10},{10,8},{9,1... | collective-permute-start | bytes 14155784 | tf_op jit(solution)/shard_map/ppermute | solution.py:260
  2.3 19.9 %collective-permute-start.4 = (f32[512,2304]{1,0:T(8,128)}, f32[512,2304]{1,0:T(8,128)S(1)}, u32[]{:S(2)}, u32[]{:S(2)}) collective-permute-start(f32[512,2304]{1,0:T(8,128)} %param.10), channel_id=1, source_target_pairs={{0,2},{2,0},{1,3},{3,1},{4,6},{6,4},{5,7},{7,5},{8,10},{10,8},{9,1... | collective-permute-start | bytes 14155784 | tf_op jit(solution)/shard_map/ppermute | solution.py:260
  2.4 9.7 %collective-permute-start.1 = (f32[16,2304]{1,0:T(8,128)S(1)}, f32[16,2304]{1,0:T(8,128)S(1)}, u32[]{:S(2)}, u32[]{:S(2)}) collective-permute-start(f32[16,2304]{1,0:T(8,128)S(1)} %get-tuple-element.1204), channel_id=1, source_target_pairs={{0,8},{8,16},{16,24},{24,0},{1,9},{9,17},{17,25},{25,1},{2,10},{10... | collective-permute-start | bytes 442376 | tf_op jit(solution)/shard_map/ppermute | solution.py:273
  7.5 11.3 %collective-permute-start.6 = (f32[16,2304]{1,0:T(8,128)S(1)}, f32[16,2304]{1,0:T(8,128)S(1)}, u32[]{:S(2)}, u32[]{:S(2)}) collective-permute-start(f32[16,2304]{1,0:T(8,128)S(1)} %get-tuple-element.1257), channel_id=1, source_target_pairs={{0,8},{8,16},{16,24},{24,0},{1,9},{9,17},{17,25},{25,1},{2,10},{10... | collective-permute-start | bytes 442376 | tf_op jit(solution)/shard_map/ppermute | solution.py:273
  12.1 15.4 %collective-permute-start = (f32[2,512]{1,0:T(2,128)S(1)}, f32[2,512]{1,0:T(2,128)S(1)}, u32[]{:S(2)}, u32[]{:S(2)}) collective-permute-start(f32[2,512]{1,0:T(2,128)S(1)} %pad_maximum_fusion.22), channel_id=1, source_target_pairs={{0,2},{2,0},{1,3},{3,1},{4,6},{6,4},{5,7},{7,5},{8,10},{10,8},{9,1... | collective-permute-start | bytes 12296 | tf_op jit(solution)/shard_map/ppermute | solution.py:260
  27.5 10.1 %collective-permute-start.10 = (f32[16,2304]{1,0:T(8,128)S(1)}, f32[16,2304]{1,0:T(8,128)S(1)}, u32[]{:S(2)}, u32[]{:S(2)}) collective-permute-start(f32[16,2304]{1,0:T(8,128)S(1)} %collective-permute-done.6), channel_id=1, source_target_pairs={{0,8},{8,16},{16,24},{24,0},{1,9},{9,17},{17,25},{25,1},{2,10},{10... | collective-permute-start | bytes 442376 | tf_op jit(solution)/shard_map/ppermute | solution.py:273
  27.6 20.2 %collective-permute-start.8 = (f32[64,2304]{1,0:T(8,128)S(1)}, f32[64,2304]{1,0:T(8,128)S(1)}, u32[]{:S(2)}, u32[]{:S(2)}) collective-permute-start(f32[64,2304]{1,0:T(8,128)S(1)} %pad_maximum_fusion.12.first), channel_id=1, source_target_pairs={{0,4},{4,0},{1,5},{5,1},{2,6},{6,2},{3,7},{7,3},{8,12},{12,8},{9,1... | collective-permute-start | bytes 1769480 | tf_op jit(solution)/shard_map/ppermute | solution.py:260
  29.2 12.4 %collective-permute-start.13 = (f32[16,2304]{1,0:T(8,128)S(1)}, f32[16,2304]{1,0:T(8,128)S(1)}, u32[]{:S(2)}, u32[]{:S(2)}) collective-permute-start(f32[16,2304]{1,0:T(8,128)S(1)} %get-tuple-element.1337), channel_id=1, source_target_pairs={{0,24},{8,0},{16,8},{24,16},{1,25},{9,1},{17,9},{25,17},{2,26},{10... | collective-permute-start | bytes 442376 | tf_op jit(solution)/shard_map/ppermute | solution.py:273
  37.6 9.5 %collective-permute-start.11 = (f32[16,2304]{1,0:T(8,128)S(1)}, f32[16,2304]{1,0:T(8,128)S(1)}, u32[]{:S(2)}, u32[]{:S(2)}) collective-permute-start(f32[16,2304]{1,0:T(8,128)S(1)} %get-tuple-element.1394), channel_id=1, source_target_pairs={{0,24},{8,0},{16,8},{24,16},{1,25},{9,1},{17,9},{25,17},{2,26},{10... | collective-permute-start | bytes 442376 | tf_op jit(solution)/shard_map/ppermute | solution.py:273
  41.6 14.3 %collective-permute-start.15 = (f32[64,2304]{1,0:T(8,128)S(1)}, f32[64,2304]{1,0:T(8,128)S(1)}, u32[]{:S(2)}, u32[]{:S(2)}) collective-permute-start(f32[64,2304]{1,0:T(8,128)S(1)} %pad_maximum_fusion.13.first), channel_id=1, source_target_pairs={{0,4},{4,0},{1,5},{5,1},{2,6},{6,2},{3,7},{7,3},{8,12},{12,8},{9,1... | collective-permute-start | bytes 1769480 | tf_op jit(solution)/shard_map/ppermute | solution.py:260
  49.9 14.9 %collective-permute-start.14 = (f32[128,1024]{1,0:T(8,128)S(1)}, f32[128,1024]{1,0:T(8,128)S(1)}, u32[]{:S(2)}, u32[]{:S(2)}) collective-permute-start(f32[128,1024]{1,0:T(8,128)S(1)} %shard_map.101.refs_0_), channel_id=1, source_target_pairs={{0,1},{1,0},{2,3},{3,2},{4,5},{5,4},{6,7},{7,6},{8,9},{9,8},{10,11... | collective-permute-start | bytes 1572872 | tf_op jit(solution)/shard_map/ppermute | solution.py:260
  54.3 23.2 %collective-permute-start.21 = (f32[128,2304]{1,0:T(8,128)S(1)}, f32[128,2304]{1,0:T(8,128)S(1)}, u32[]{:S(2)}, u32[]{:S(2)}) collective-permute-start(f32[128,2304]{1,0:T(8,128)S(1)} %pad_maximum_fusion.refs_0_), channel_id=1, source_target_pairs={{0,2},{2,0},{1,3},{3,1},{4,6},{6,4},{5,7},{7,5},{8,10},{10,8},{9,1... | collective-permute-start | bytes 3538952 | tf_op jit(solution)/shard_map/ppermute | solution.py:260
  54.4 15.8 %collective-permute-start.18 = (f32[64,2304]{1,0:T(8,128)S(1)}, f32[64,2304]{1,0:T(8,128)S(1)}, u32[]{:S(2)}, u32[]{:S(2)}) collective-permute-start(f32[64,2304]{1,0:T(8,128)S(1)} %pad_maximum_fusion.14.first), channel_id=1, source_target_pairs={{0,4},{4,0},{1,5},{5,1},{2,6},{6,2},{3,7},{7,3},{8,12},{12,8},{9,1... | collective-permute-start | bytes 1769480 | tf_op jit(solution)/shard_map/ppermute | solution.py:260
  57.9 16.7 %collective-permute-start.20 = (f32[128,1024]{1,0:T(8,128)S(1)}, f32[128,1024]{1,0:T(8,128)S(1)}, u32[]{:S(2)}, u32[]{:S(2)}) collective-permute-start(f32[128,1024]{1,0:T(8,128)S(1)} %shard_map.102.refs_0_), channel_id=1, source_target_pairs={{0,1},{1,0},{2,3},{3,2},{4,5},{5,4},{6,7},{7,6},{8,9},{9,8},{10,11... | collective-permute-start | bytes 1572872 | tf_op jit(solution)/shard_map/ppermute | solution.py:260
  66.9 21.8 %collective-permute-start.25 = (f32[128,2304]{1,0:T(8,128)S(1)}, f32[128,2304]{1,0:T(8,128)S(1)}, u32[]{:S(2)}, u32[]{:S(2)}) collective-permute-start(f32[128,2304]{1,0:T(8,128)S(1)} %pad_maximum_fusion.1.refs_1_), channel_id=1, source_target_pairs={{0,2},{2,0},{1,3},{3,1},{4,6},{6,4},{5,7},{7,5},{8,10},{10,8},{9,1... | collective-permute-start | bytes 3538952 | tf_op jit(solution)/shard_map/ppermute | solution.py:260
  67.0 15.8 %collective-permute-start.22 = (f32[64,2304]{1,0:T(8,128)S(1)}, f32[64,2304]{1,0:T(8,128)S(1)}, u32[]{:S(2)}, u32[]{:S(2)}) collective-permute-start(f32[64,2304]{1,0:T(8,128)S(1)} %pad_maximum_fusion.15.first), channel_id=1, source_target_pairs={{0,4},{4,0},{1,5},{5,1},{2,6},{6,2},{3,7},{7,3},{8,12},{12,8},{9,1... | collective-permute-start | bytes 1769480 | tf_op jit(solution)/shard_map/ppermute | solution.py:260
  72.1 13.7 %collective-permute-start.23 = (f32[128,1024]{1,0:T(8,128)S(1)}, f32[128,1024]{1,0:T(8,128)S(1)}, u32[]{:S(2)}, u32[]{:S(2)}) collective-permute-start(f32[128,1024]{1,0:T(8,128)S(1)} %shard_map.104.refs_0_), channel_id=1, source_target_pairs={{0,1},{1,0},{2,3},{3,2},{4,5},{5,4},{6,7},{7,6},{8,9},{9,8},{10,11... | collective-permute-start | bytes 1572872 | tf_op jit(solution)/shard_map/ppermute | solution.py:260
  74.6 13.3 %collective-permute-start.24 = (f32[128,512]{1,0:T(8,128)S(1)}, f32[128,512]{1,0:T(8,128)S(1)}, u32[]{:S(2)}, u32[]{:S(2)}) collective-permute-start(f32[128,512]{1,0:T(8,128)S(1)} %get-tuple-element.975), channel_id=1, source_target_pairs={{0,2},{2,0},{1,3},{3,1},{4,6},{6,4},{5,7},{7,5},{8,10},{10,8},{9,1... | collective-permute-start | bytes 786440 | tf_op jit(solution)/shard_map/ppermute | solution.py:260
  89.3 16.2 %collective-permute-start.19 = (f32[64,2304]{1,0:T(8,128)S(1)}, f32[64,2304]{1,0:T(8,128)S(1)}, u32[]{:S(2)}, u32[]{:S(2)}) collective-permute-start(f32[64,2304]{1,0:T(8,128)S(1)} %get-tuple-element.988), channel_id=1, source_target_pairs={{0,4},{4,0},{1,5},{5,1},{2,6},{6,2},{3,7},{7,3},{8,12},{12,8},{9,1... | collective-permute-start | bytes 1769480 | tf_op jit(solution)/shard_map/ppermute | solution.py:260
  90.8 20.0 %collective-permute-start.30 = (f32[128,512]{1,0:T(8,128)S(1)}, f32[128,512]{1,0:T(8,128)S(1)}, u32[]{:S(2)}, u32[]{:S(2)}) collective-permute-start(f32[128,512]{1,0:T(8,128)S(1)} %get-tuple-element.1030), channel_id=1, source_target_pairs={{0,2},{2,0},{1,3},{3,1},{4,6},{6,4},{5,7},{7,5},{8,10},{10,8},{9,1... | collective-permute-start | bytes 786440 | tf_op jit(solution)/shard_map/ppermute | solution.py:260
  90.8 14.8 %collective-permute-start.29 = (f32[128,1024]{1,0:T(8,128)S(1)}, f32[128,1024]{1,0:T(8,128)S(1)}, u32[]{:S(2)}, u32[]{:S(2)}) collective-permute-start(f32[128,1024]{1,0:T(8,128)S(1)} %shard_map.106.refs_0_), channel_id=1, source_target_pairs={{0,1},{1,0},{2,3},{3,2},{4,5},{5,4},{6,7},{7,6},{8,9},{9,8},{10,11... | collective-permute-start | bytes 1572872 | tf_op jit(solution)/shard_map/ppermute | solution.py:260
  92.3 18.5 %collective-permute-start.31 = (f32[128,512]{1,0:T(8,128)S(1)}, f32[128,512]{1,0:T(8,128)S(1)}, u32[]{:S(2)}, u32[]{:S(2)}) collective-permute-start(f32[128,512]{1,0:T(8,128)S(1)} %get-tuple-element.1096), channel_id=1, source_target_pairs={{0,2},{2,0},{1,3},{3,1},{4,6},{6,4},{5,7},{7,5},{8,10},{10,8},{9,1... | collective-permute-start | bytes 786440 | tf_op jit(solution)/shard_map/ppermute | solution.py:260
  93.3 25.2 %collective-permute-start.35 = (f32[64,2304]{1,0:T(8,128)S(1)}, f32[64,2304]{1,0:T(8,128)S(1)}, u32[]{:S(2)}, u32[]{:S(2)}) collective-permute-start(f32[64,2304]{1,0:T(8,128)S(1)} %get-tuple-element.1119), channel_id=1, source_target_pairs={{0,4},{4,0},{1,5},{5,1},{2,6},{6,2},{3,7},{7,3},{8,12},{12,8},{9,1... | collective-permute-start | bytes 1769480 | tf_op jit(solution)/shard_map/ppermute | solution.py:260
  110.8 23.6 %collective-permute-start.38 = (f32[64,2304]{1,0:T(8,128)S(1)}, f32[64,2304]{1,0:T(8,128)S(1)}, u32[]{:S(2)}, u32[]{:S(2)}) collective-permute-start(f32[64,2304]{1,0:T(8,128)S(1)} %get-tuple-element.1123), channel_id=1, source_target_pairs={{0,4},{4,0},{1,5},{5,1},{2,6},{6,2},{3,7},{7,3},{8,12},{12,8},{9,1... | collective-permute-start | bytes 1769480 | tf_op jit(solution)/shard_map/ppermute | solution.py:260
  121.2 12.4 %collective-permute-start.39 = (f32[16,2304]{1,0:T(8,128)S(1)}, f32[16,2304]{1,0:T(8,128)S(1)}, u32[]{:S(2)}, u32[]{:S(2)}) collective-permute-start(f32[16,2304]{1,0:T(8,128)S(1)} %get-tuple-element.1216), channel_id=1, source_target_pairs={{0,8},{8,16},{16,24},{24,0},{1,9},{9,17},{17,25},{25,1},{2,10},{10... | collective-permute-start | bytes 442376 | tf_op jit(solution)/shard_map/ppermute | solution.py:273
  123.2 36.4 %collective-permute-start.45 = (f32[64,2304]{1,0:T(8,128)S(1)}, f32[64,2304]{1,0:T(8,128)S(1)}, u32[]{:S(2)}, u32[]{:S(2)}) collective-permute-start(f32[64,2304]{1,0:T(8,128)S(1)} %get-tuple-element.1277), channel_id=1, source_target_pairs={{0,4},{4,0},{1,5},{5,1},{2,6},{6,2},{3,7},{7,3},{8,12},{12,8},{9,1... | collective-permute-start | bytes 1769480 | tf_op jit(solution)/shard_map/ppermute | solution.py:260
  127.8 10.0 %collective-permute-start.37 = (f32[16,2304]{1,0:T(8,128)S(1)}, f32[16,2304]{1,0:T(8,128)S(1)}, u32[]{:S(2)}, u32[]{:S(2)}) collective-permute-start(f32[16,2304]{1,0:T(8,128)S(1)} %add_subtract_fusion.3), channel_id=1, source_target_pairs={{0,8},{8,16},{16,24},{24,0},{1,9},{9,17},{17,25},{25,1},{2,10},{10... | collective-permute-start | bytes 442376 | tf_op jit(solution)/shard_map/ppermute | solution.py:273
  146.1 13.6 %collective-permute-start.46 = (f32[16,2304]{1,0:T(8,128)S(1)}, f32[16,2304]{1,0:T(8,128)S(1)}, u32[]{:S(2)}, u32[]{:S(2)}) collective-permute-start(f32[16,2304]{1,0:T(8,128)S(1)} %get-tuple-element.1294), channel_id=1, source_target_pairs={{0,8},{8,16},{16,24},{24,0},{1,9},{9,17},{17,25},{25,1},{2,10},{10... | collective-permute-start | bytes 442376 | tf_op jit(solution)/shard_map/ppermute | solution.py:273
  158.0 11.2 %collective-permute-start.44 = (f32[64,2304]{1,0:T(8,128)S(1)}, f32[64,2304]{1,0:T(8,128)S(1)}, u32[]{:S(2)}, u32[]{:S(2)}) collective-permute-start(f32[64,2304]{1,0:T(8,128)S(1)} %pad_maximum_fusion.16.first), channel_id=1, source_target_pairs={{0,4},{4,0},{1,5},{5,1},{2,6},{6,2},{3,7},{7,3},{8,12},{12,8},{9,1... | collective-permute-start | bytes 1769480 | tf_op jit(solution)/shard_map/ppermute | solution.py:260
  162.7 9.4 %collective-permute-start.51 = (f32[16,2304]{1,0:T(8,128)S(1)}, f32[16,2304]{1,0:T(8,128)S(1)}, u32[]{:S(2)}, u32[]{:S(2)}) collective-permute-start(f32[16,2304]{1,0:T(8,128)S(1)} %add.187), channel_id=1, source_target_pairs={{0,24},{8,0},{16,8},{24,16},{1,25},{9,1},{17,9},{25,17},{2,26},{10... | collective-permute-start | bytes 442376 | tf_op jit(solution)/shard_map/ppermute | solution.py:273
  163.5 9.5 %collective-permute-start.50 = (f32[16,2304]{1,0:T(8,128)S(1)}, f32[16,2304]{1,0:T(8,128)S(1)}, u32[]{:S(2)}, u32[]{:S(2)}) collective-permute-start(f32[16,2304]{1,0:T(8,128)S(1)} %collective-permute-done.49), channel_id=1, source_target_pairs={{0,8},{8,16},{16,24},{24,0},{1,9},{9,17},{17,25},{25,1},{2,10},{10... | collective-permute-start | bytes 442376 | tf_op jit(solution)/shard_map/ppermute | solution.py:273
  168.4 11.2 %collective-permute-start.52 = (f32[16,2304]{1,0:T(8,128)S(1)}, f32[16,2304]{1,0:T(8,128)S(1)}, u32[]{:S(2)}, u32[]{:S(2)}) collective-permute-start(f32[16,2304]{1,0:T(8,128)S(1)} %get-tuple-element.1356), channel_id=1, source_target_pairs={{0,8},{8,16},{16,24},{24,0},{1,9},{9,17},{17,25},{25,1},{2,10},{10... | collective-permute-start | bytes 442376 | tf_op jit(solution)/shard_map/ppermute | solution.py:273
  173.0 9.5 %collective-permute-start.56 = (f32[16,2304]{1,0:T(8,128)S(1)}, f32[16,2304]{1,0:T(8,128)}, u32[]{:S(2)}, u32[]{:S(2)}) collective-permute-start(f32[16,2304]{1,0:T(8,128)S(1)} %add_subtract_fusion.1), channel_id=1, source_target_pairs={{0,8},{8,16},{16,24},{24,0},{1,9},{9,17},{17,25},{25,1},{2,10},{10... | collective-permute-start | bytes 442376 | tf_op jit(solution)/shard_map/ppermute | solution.py:273
  173.9 10.3 %collective-permute-start.54 = (f32[128,1024]{1,0:T(8,128)S(1)}, f32[128,1024]{1,0:T(8,128)S(1)}, u32[]{:S(2)}, u32[]{:S(2)}) collective-permute-start(f32[128,1024]{1,0:T(8,128)S(1)} %shard_map.111), channel_id=1, source_target_pairs={{0,1},{1,0},{2,3},{3,2},{4,5},{5,4},{6,7},{7,6},{8,9},{9,8},{10,11... | collective-permute-start | bytes 1572872 | tf_op jit(solution)/shard_map/ppermute | solution.py:260
  180.9 11.9 %collective-permute-start.53 = (f32[64,2304]{1,0:T(8,128)S(1)}, f32[64,2304]{1,0:T(8,128)S(1)}, u32[]{:S(2)}, u32[]{:S(2)}) collective-permute-start(f32[64,2304]{1,0:T(8,128)S(1)} %pad_maximum_fusion.17.first), channel_id=1, source_target_pairs={{0,4},{4,0},{1,5},{5,1},{2,6},{6,2},{3,7},{7,3},{8,12},{12,8},{9,1... | collective-permute-start | bytes 1769480 | tf_op jit(solution)/shard_map/ppermute | solution.py:260
  183.2 17.5 %collective-permute-start.59 = (f32[16,2304]{1,0:T(8,128)}, f32[16,2304]{1,0:T(8,128)}, u32[]{:S(2)}, u32[]{:S(2)}) collective-permute-start(f32[16,2304]{1,0:T(8,128)} %collective-permute-done.56), channel_id=1, source_target_pairs={{0,8},{8,16},{16,24},{24,0},{1,9},{9,17},{17,25},{25,1},{2,10},{10... | collective-permute-start | bytes 442376 | tf_op jit(solution)/shard_map/ppermute | solution.py:273
  187.0 18.2 %collective-permute-start.62 = (f32[16,2304]{1,0:T(8,128)}, f32[16,2304]{1,0:T(8,128)}, u32[]{:S(2)}, u32[]{:S(2)}) collective-permute-start(f32[16,2304]{1,0:T(8,128)} %add_subtract_fusion), channel_id=1, source_target_pairs={{0,8},{8,16},{16,24},{24,0},{1,9},{9,17},{17,25},{25,1},{2,10},{10... | collective-permute-start | bytes 442376 | tf_op jit(solution)/shard_map/ppermute | solution.py:273
  187.0 18.6 %collective-permute-start.64 = (f32[16,2304]{1,0:T(8,128)}, f32[16,2304]{1,0:T(8,128)}, u32[]{:S(2)}, u32[]{:S(2)}) collective-permute-start(f32[16,2304]{1,0:T(8,128)} %add_subtract_fusion), channel_id=1, source_target_pairs={{0,24},{8,0},{16,8},{24,16},{1,25},{9,1},{17,9},{25,17},{2,26},{10... | collective-permute-start | bytes 442376 | tf_op jit(solution)/shard_map/ppermute | solution.py:273
  203.1 13.8 %collective-permute-start.61 = (f32[128,1024]{1,0:T(8,128)S(1)}, f32[128,1024]{1,0:T(8,128)S(1)}, u32[]{:S(2)}, u32[]{:S(2)}) collective-permute-start(f32[128,1024]{1,0:T(8,128)S(1)} %shard_map.112), channel_id=1, source_target_pairs={{0,1},{1,0},{2,3},{3,2},{4,5},{5,4},{6,7},{7,6},{8,9},{9,8},{10,11... | collective-permute-start | bytes 1572872 | tf_op jit(solution)/shard_map/ppermute | solution.py:260
  205.6 16.9 %collective-permute-start.60 = (f32[64,2304]{1,0:T(8,128)S(1)}, f32[64,2304]{1,0:T(8,128)}, u32[]{:S(2)}, u32[]{:S(2)}) collective-permute-start(f32[64,2304]{1,0:T(8,128)S(1)} %pad_maximum_fusion.18.first), channel_id=1, source_target_pairs={{0,4},{4,0},{1,5},{5,1},{2,6},{6,2},{3,7},{7,3},{8,12},{12,8},{9,1... | collective-permute-start | bytes 1769480 | tf_op jit(solution)/shard_map/ppermute | solution.py:260
  217.7 19.8 %collective-permute-start.66 = (f32[64,2304]{1,0:T(8,128)S(1)}, f32[64,2304]{1,0:T(8,128)}, u32[]{:S(2)}, u32[]{:S(2)}) collective-permute-start(f32[64,2304]{1,0:T(8,128)S(1)} %pad_maximum_fusion.19.first), channel_id=1, source_target_pairs={{0,4},{4,0},{1,5},{5,1},{2,6},{6,2},{3,7},{7,3},{8,12},{12,8},{9,1... | collective-permute-start | bytes 1769480 | tf_op jit(solution)/shard_map/ppermute | solution.py:260
  231.5 14.0 %collective-permute-start.67 = (f32[128,1024]{1,0:T(8,128)S(1)}, f32[128,1024]{1,0:T(8,128)S(1)}, u32[]{:S(2)}, u32[]{:S(2)}) collective-permute-start(f32[128,1024]{1,0:T(8,128)S(1)} %shard_map.113), channel_id=1, source_target_pairs={{0,1},{1,0},{2,3},{3,2},{4,5},{5,4},{6,7},{7,6},{8,9},{9,8},{10,11... | collective-permute-start | bytes 1572872 | tf_op jit(solution)/shard_map/ppermute | solution.py:260
  232.7 14.2 %collective-permute-start.69 = (f32[128,2304]{1,0:T(8,128)S(1)}, f32[128,2304]{1,0:T(8,128)S(1)}, u32[]{:S(2)}, u32[]{:S(2)}) collective-permute-start(f32[128,2304]{1,0:T(8,128)S(1)} %copy-done.15), channel_id=1, source_target_pairs={{0,2},{2,0},{1,3},{3,1},{4,6},{6,4},{5,7},{7,5},{8,10},{10,8},{9,1... | collective-permute-start | bytes 3538952 | tf_op jit(solution)/shard_map/ppermute | solution.py:260
  232.7 19.9 %collective-permute-start.71 = (f32[128,2304]{1,0:T(8,128)}, f32[128,2304]{1,0:T(8,128)}, u32[]{:S(2)}, u32[]{:S(2)}) collective-permute-start(f32[128,2304]{1,0:T(8,128)} %pad_maximum_fusion.6.refs_1_), channel_id=1, source_target_pairs={{0,2},{2,0},{1,3},{3,1},{4,6},{6,4},{5,7},{7,5},{8,10},{10,8},{9,1... | collective-permute-start | bytes 3538952 | tf_op jit(solution)/shard_map/ppermute | solution.py:260
  242.3 10.3 %collective-permute-start.72 = (f32[128,2304]{1,0:T(8,128)}, f32[128,2304]{1,0:T(8,128)}, u32[]{:S(2)}, u32[]{:S(2)}) collective-permute-start(f32[128,2304]{1,0:T(8,128)} %pad_maximum_fusion.8.refs_2_), channel_id=1, source_target_pairs={{0,2},{2,0},{1,3},{3,1},{4,6},{6,4},{5,7},{7,5},{8,10},{10,8},{9,1... | collective-permute-start | bytes 3538952 | tf_op jit(solution)/shard_map/ppermute | solution.py:260
  242.3 26.1 %collective-permute-start.74 = (f32[128,1024]{1,0:T(8,128)}, f32[128,1024]{1,0:T(8,128)}, u32[]{:S(2)}, u32[]{:S(2)}) collective-permute-start(f32[128,1024]{1,0:T(8,128)} %shard_map.114), channel_id=1, source_target_pairs={{0,1},{1,0},{2,3},{3,2},{4,5},{5,4},{6,7},{7,6},{8,9},{9,8},{10,11... | collective-permute-start | bytes 1572872 | tf_op jit(solution)/shard_map/ppermute | solution.py:260
  252.5 15.8 %collective-permute-start.70 = (f32[2,2304]{1,0:T(2,128)S(1)}, f32[2,2304]{1,0:T(2,128)S(1)}, u32[]{:S(2)}, u32[]{:S(2)}) collective-permute-start(f32[2,2304]{1,0:T(2,128)S(1)} %pad_maximum_fusion.20), channel_id=1, source_target_pairs={{0,2},{2,0},{1,3},{3,1},{4,6},{6,4},{5,7},{7,5},{8,10},{10,8},{9,1... | collective-permute-start | bytes 55304 | tf_op jit(solution)/shard_map/ppermute | solution.py:260
  271.0 15.9 %collective-permute-start.75 = (f32[1]{0:T(128)}, f32[1]{0:T(128)}, u32[]{:S(2)}, u32[]{:S(2)}) collective-permute-start(f32[1]{0:T(128)} %bitcast.10), channel_id=1, source_target_pairs={{0,1},{1,0},{2,3},{3,2},{4,5},{5,4},{6,7},{7,6},{8,9},{9,8},{10,11... | collective-permute-start | bytes 20 | tf_op jit(solution)/shard_map/ppermute | solution.py:260
  (74 other events, 838.2 us)

commit v2 on v1

--- a/solution.py
+++ b/solution.py
@@ -39,8 +39,13 @@
         at += x.shape[0]
 
 
-def product_kernel(dims, first, second, own_high, own_low, far_high, far_low, out, stack):
+def product_kernel(dims, slots, first, second, own_high, own_low, far_high, far_low, out, *rest):
+    *stats, stack = rest
     fill(stack, first[...], second[...])
+    for n, rows in enumerate((first, second) if slots else ()):
+        blocks = rows[...].reshape(slots, rows.shape[0] // slots, rows.shape[1])
+        stats[0][0, n * slots : (n + 1) * slots] = jnp.sum(blocks, axis=1)
+        stats[0][1, n * slots : (n + 1) * slots] = jnp.sum(blocks * blocks, axis=1)
     latents = out.shape[1] // 2
     out[:, :latents] = stacked_dot(stack, own_high, own_low, dims)
     out[:, latents:] = stacked_dot(stack, far_high, far_low, dims)
@@ -50,16 +55,19 @@
 COST = pl.CostEstimate(flops=1, bytes_accessed=1, transcendentals=0)
 
 
-def product(first, second, weights, dims):
+def product(first, second, weights, dims, slots=0):
     latents = weights[0].shape[0 if dims == ROWS_BY_ROWS else 1]
     depth = first.shape[1]
     rows = first.shape[0] + second.shape[0]
     whole = pl.BlockSpec(memory_space=pltpu.VMEM)
+    shapes = [jax.ShapeDtypeStruct((rows, 2 * latents), jnp.float32)]
+    if slots:
+        shapes.append(jax.ShapeDtypeStruct((2, 2 * slots, depth), jnp.float32))
     return pl.pallas_call(
-        functools.partial(product_kernel, dims),
-        out_shape=jax.ShapeDtypeStruct((rows, 2 * latents), jnp.float32),
+        functools.partial(product_kernel, dims, slots),
+        out_shape=shapes,
         in_specs=[whole] * 6,
-        out_specs=whole,
+        out_specs=[whole] * len(shapes),
         scratch_shapes=[pltpu.VMEM((2 * rows, depth), jnp.bfloat16)],
         compiler_params=PARAMS,
         cost_estimate=COST,
@@ -127,49 +135,50 @@
     )(*parts)
 
 
-def grad_kernel(scale, by_rows, tile, left_high, left_low, *refs):
-    *pieces, out, high, low, result, sems = refs
-
-    def fill_right(cut):
+def grad_kernel(scale, near_high, near_low, far_high, far_low, *refs):
+    *pieces, out, bias, high, low = refs
+
+    @pl.when(pl.program_id(1) == 0)
+    def _():
         at = 0
         for p in pieces:
             rows = p.shape[0]
-            high[at : at + rows], low[at : at + rows] = split_bf16(p[:, cut])
+            high[at : at + rows], low[at : at + rows] = split_bf16(p[...])
             at += rows
+        bias[...] = sum(jnp.sum(p[...], axis=0, keepdims=True) for p in pieces)
 
     def part(a, b):
-        return jnp.dot(a, b[...], preferred_element_type=jnp.float32)
-
-    copies = []
-    for n, at in enumerate(range(0, out.shape[0 if by_rows else 1], tile)):
-        cut = slice(at, at + tile)
-        rows, columns = (cut, slice(None)) if by_rows else (slice(None), cut)
-        if n == 0 or not by_rows:
-            fill_right(columns)
-        total = part(left_high[rows], high) + part(left_high[rows], low) + part(left_low[rows], high)
-        result[rows, columns] = total * scale
-        copies.append(pltpu.make_async_copy(result.at[rows, columns], out.at[rows, columns], sems.at[n]))
-        copies[-1].start()
-    for copy in copies:
-        copy.wait()
-
-
-def grad(left, pieces, scale, by_rows):
-    rows, depth = left[0].shape
+        return jnp.dot(a[...], b, preferred_element_type=jnp.float32)
+
+    half = near_high.shape[1]
+    total = part(near_high, high[:half]) + part(far_high, high[half:])
+    total += part(near_high, low[:half]) + part(far_high, low[half:])
+    total += part(near_low, high[:half]) + part(far_low, high[half:])
+    out[...] = total * scale
+
+
+def grad(near, far, near_pieces, far_pieces, scale, by_rows):
+    rows, half = near[0].shape
+    pieces = [*near_pieces, *far_pieces]
     columns = pieces[0].shape[1]
-    split = rows if by_rows else columns
-    tile = TILE if split % TILE == 0 else split
-    shape = (rows, columns)
+    if by_rows:
+        tm, tn = TILE if rows % TILE == 0 else rows, columns
+    else:
+        tm, tn = rows, TILE if columns % TILE == 0 else columns
     return pl.pallas_call(
-        functools.partial(grad_kernel, scale, by_rows, tile),
-        out_shape=jax.ShapeDtypeStruct(shape, jnp.float32),
-        in_specs=[pl.BlockSpec(memory_space=pltpu.VMEM)] * (2 + len(pieces)),
-        out_specs=pl.BlockSpec(memory_space=pl.ANY),
-        scratch_shapes=[pltpu.VMEM((depth, columns if by_rows else tile), jnp.bfloat16)] * 2
-        + [pltpu.VMEM(shape, jnp.float32), pltpu.SemaphoreType.DMA((split // tile,))],
-        compiler_params=pltpu.CompilerParams(vmem_limit_bytes=24 * 1024 * 1024),
+        functools.partial(grad_kernel, scale),
+        out_shape=(
+            jax.ShapeDtypeStruct((rows, columns), jnp.float32),
+            jax.ShapeDtypeStruct((1, columns), jnp.float32),
+        ),
+        grid=(columns // tn, rows // tm),
+        in_specs=[pl.BlockSpec((tm, half), lambda j, i: (i, 0))] * 4
+        + [pl.BlockSpec((p.shape[0], tn), lambda j, i: (0, j)) for p in pieces],
+        out_specs=(pl.BlockSpec((tm, tn), lambda j, i: (i, j)), pl.BlockSpec((1, tn), lambda j, i: (0, j))),
+        scratch_shapes=[pltpu.VMEM((2 * half, tn), jnp.bfloat16)] * 2,
+        compiler_params=pltpu.CompilerParams(vmem_limit_bytes=56 * 1024 * 1024),
         cost_estimate=COST,
-    )(*left, *pieces)
+    )(*near, *far, *pieces)
 
 
 class Step:
@@ -326,10 +335,6 @@
         high = lax.reduce_precision(x, 8, 7)
         return high.astype(jnp.bfloat16), (x - high).astype(jnp.bfloat16)
 
-    def sums(a, b):
-        blocks = jnp.concatenate([a, b], axis=0).reshape(lat // 2, -1, width)
-        return jnp.sum(blocks, axis=1), jnp.sum(blocks * blocks, axis=1)
-
     chunks, at = [], 0
     for k, piece in enumerate(pieces):
         chunks.append(plan.add("tc", 0.2, -10.0 + k, lambda a=at, b=at + piece: acts[a:b]))
@@ -350,8 +355,7 @@
     def half(n):
         return lambda xs: xs[n]
 
-    count = len(pieces)
-    totals, biases, gates, rows, rows_far, feats_far = [], [], [], [], [], []
+    totals, gates, rows, rows_far, feats_far = [], [], [], [], []
     errs, errs_far, dpres, dpres_far = [], [], [], []
     for k, (own, piece) in enumerate(zip(chunks, pieces)):
         ranks = [2.0 * k - 2.5 * stage for stage in range(5)]
@@ -360,7 +364,7 @@
         part_cost = 2 * piece * lat * latents * 4 / 70e3
         near, far = gather(own, piece, ranks[0])
         part = plan.add(
-            "tc", 3.6, ranks[1], lambda a, b, *w: product(a, b, w[0] + w[1], ROWS_BY_COLS), near, far, *enc_parts
+            "tc", 3.6, ranks[1], lambda a, b, *w: product(a, b, w[0] + w[1], ROWS_BY_COLS)[0], near, far, *enc_parts
         )
         parts = sum_wid(part, ranks[1], part_cost)
         gated = plan.add("tc", 3.6, ranks[1], lambda l, v, w, *ps: gate(ps, l, v + w), limits, *dec_parts, *parts)
@@ -369,39 +373,44 @@
             "tc", 0.8, ranks[3], lambda s, u, d, a: ((s[0] + u) + d) + dec_bias[None, :] - a, line, up, down, own
         )
         err_near, err_far = gather(err, piece, ranks[3])
-        back = plan.add(
-            "tc", 3.6, ranks[4], lambda a, b, *w: product(a, b, w[0] + w[1], ROWS_BY_ROWS), err_near, err_far, *dec_parts
+        both = plan.add(
+            "tc", 3.6, ranks[4], lambda a, b, *w: product(a, b, w[0] + w[1], ROWS_BY_ROWS, long), err_near, err_far, *dec_parts
         )
+        back = plan.add("tc", 0.0, ranks[4], lambda x: x[0], both)
+        totals.append(both)
         total = sum_wid(back, ranks[4], part_cost)
         dpre = plan.add("tc", 0.9, ranks[4], slopes, gated, *total)
         dpre_far = plan.add("core", 0.5 * size, ranks[4], lambda d: swap("core")(d[1]), dpre)
 
         pair = plan.add("tc", 0.9 * size, late, cat, near, far)
-        rows.append(pair)
         rows_far.append(plan.add("core", 2.0 * size, late, swap("core"), pair))
         feats_far.append(plan.add("core", 0.5 * size, late, lambda g: swap("core")(g[2]), gated))
         pair = plan.add("tc", 0.9 * size, late, cat, err_near, err_far)
         errs_far.append(plan.add("core", 2.0 * size, late, swap("core"), pair))
-        errs.append(pair)
+        rows += [near, far]
+        errs += [err_near, err_far]
         gates.append(gated)
         dpres.append(dpre)
         dpres_far.append(dpre_far)
-        totals.append(plan.add("tc", 1.0, late + 3, sums, err_near, err_far))
-        biases.append(plan.add("tc", 0.6, late + 4, lambda d, f: (jnp.sum(d[0], axis=0), jnp.sum(f, axis=0)), dpre, dpre_far))
-
-    turned_rows = plan.add("tc", 5.0, 300, turn, *rows, *rows_far)
-    turned_feats = plan.add(
-        "tc", 1.5, 302, lambda *xs: turn(*[x[1] for x in xs[:count]], *xs[count:]), *gates, *feats_far
-    )
+
+    turned = [
+        plan.add("tc", 3.5, 300, turn, *rows),
+        plan.add("tc", 3.5, 301, turn, *rows_far),
+        plan.add("tc", 1.0, 302, lambda *gs: turn(*[g[1] for g in gs]), *gates),
+        plan.add("tc", 1.0, 303, turn, *feats_far),
+    ]
+    count = len(pieces)
     dec_sum = plan.add(
-        "tc", 8.0, 400, lambda t, *xs: grad(t, xs, total_rows**-0.5, False), turned_feats, *errs, *errs_far
+        "tc", 9.0, 400,
+        lambda n, f, *xs: grad(n, f, xs[: 2 * count], xs[2 * count :], total_rows**-0.5, False),
+        *turned[2:], *errs, *errs_far,
     )
     enc_sum = plan.add(
-        "tc", 8.0, 401,
-        lambda t, *xs: grad(t, [x[0] for x in xs[:count]] + list(xs[count:]), 1.0, True),
-        turned_rows, *dpres, *dpres_far,
+        "tc", 9.0, 401,
+        lambda n, f, *xs: grad(n, f, [x[0] for x in xs[:count]], xs[count:], 1.0, True),
+        *turned[:2], *dpres, *dpres_far,
     )
-    by_block = plan.add("tc", 0.5, 510, lambda *ts: (sum(t[0] for t in ts), sum(t[1] for t in ts)), *totals)
+    by_block = plan.add("tc", 0.5, 510, lambda *ts: sum(t[1] for t in ts), *totals)
 
     def reduced(t):
         return jnp.stack([fold(fold(x.reshape(2, long, width).swapaxes(0, 1))) for x in t])
@@ -414,8 +423,8 @@
     plan.run()
 
     loss = sum(s.value for s in squares)[0] / (total_rows * width * wid) + plan.token
-    grad_enc_bias = sum(b.value[0] for b in biases) + sum(b.value[1] for b in biases)
-    return enc_sum.value, grad_enc_bias, dec_sum.value, column.value[0] * scale, loss
+    grad_enc, grad_enc_bias = enc_sum.value
+    return grad_enc, grad_enc_bias[0], dec_sum.value[0], column.value[0] * scale, loss
 
 
 def solution(mesh):

time: 295 us -> 270 us (0.915)
  other arithmetic: 30.8 us -> 11.5 us
  local copies, waits for them, and re-layouts: 28.3 us -> 11.3 us
  starting transfers between devices: 86.2 us -> 93 us
  waiting for transfers between devices: 82.8 us -> 86.5 us
    unnamed x90 -> x54, local copies, waits for them, and re-layouts: 25.4 us -> 6.82 us
    reduce_sum x12 -> x0, other arithmetic: 12 us -> none  [the longest x4 5.61 us: sums(): return (jnp.sum(blocks, axis=1), jnp.sum(blocks * blocks, axis=1))]
    ppermute x41, waiting for transfers between devices: 22.9 us -> 32.1 us  [swap(): return lambda x: lax.ppermute(x, axis, SWAP)]
    ppermute x36, starting transfers between devices: 52 us -> 59.3 us  [shift(): lax.ppermute(x, 'z', [(i, (i + by) % long) for i in range(long)])]
    ppermute x36, waiting for transfers between devices: 60 us -> 54.4 us  [shift(): lax.ppermute(x, 'z', [(i, (i + by) % long) for i in range(long)])]
    concatenate x16, other arithmetic: 8.35 us -> 4.06 us  [cat(): return jnp.concatenate(xs, axis=0)]
    pallas_call x2 -> x4, Pallas kernels: 5.33 us -> 6 us  [turn(): pl.pallas_call(functools.partial(turn_kernel, len(parts)), out_shape=(sha...]
  transfers between devices with their start and end apart: 77 -> 77, of which waited for: 36 -> 35; matrix products, arithmetic and copies ran while one was open for 11% -> 6% of each run, Pallas kernels for 20% -> 22%
where the time goes in v2:
time: 270 us; the launch traced here: 266 us
  starting transfers between devices  93 us (34%)
  waiting for transfers between devices  86.5 us (32%)
  Pallas kernels  59.6 us (22%)
  other arithmetic  11.5 us (4%)
  local copies, waits for them, and re-layouts  11.3 us (4%)
  between operations  4.29 us (2%)
    ppermute x36, starting transfers between devices, shift(): lax.ppermute(x, 'z', [(i, (i + by) % long) for i in range(long)])  59.3 us
    ppermute x36, waiting for transfers between devices, shift(): lax.ppermute(x, 'z', [(i, (i + by) % long) for i in range(long)])  54.4 us
    ppermute x41, starting transfers between devices, swap(): return lambda x: lax.ppermute(x, axis, SWAP)  33.8 us
    ppermute x41, waiting for transfers between devices, swap(): return lambda x: lax.ppermute(x, axis, SWAP)  32.1 us
    pallas_call x2, Pallas kernels, grad(): pl.pallas_call(functools.partial(grad_kernel, scale), out_shape=(jax.Shap...  24.5 us
    pallas_call x8, Pallas kernels, product(): pl.pallas_call(functools.partial(product_kernel, dims, slots), out_shape=...  20.6 us
    pallas_call x4, Pallas kernels, gate(): pl.pallas_call(functools.partial(gate_kernel, len(parts)), out_shape=(slo...  8.47 us
    unnamed x54, local copies, waits for them, and re-layouts  6.82 us
  transfers between devices with their start and end apart: 77, of which 35 were waited for; matrix products, arithmetic and copies ran while one was open for 6% of the time, Pallas kernels for 22%

profile of v2, /device:TPU:0, one launch (start us, length us, event | category | flops | bytes accessed | tf_op | source)
XLA Modules:
  0.0 266.2 jit_solution(10999122320505859879)
XLA Ops:
  2.4 3.0 %collective-permute-start.1 = (f32[16,2304]{1,0:T(8,128)S(1)}, f32[16,2304]{1,0:T(8,128)S(1)}, u32[]{:S(2)}, u32[]{:S(2)}) collective-permute-start(f32[16,2304]{1,0:T(8,128)S(1)} %get-tuple-element.1219), channel_id=1, source_target_pairs={{0,8},{8,16},{16,24},{24,0},{1,9},{9,17},{17,25},{25,1},{2,10},{10... | collective-permute-start | bytes 442376 | tf_op jit(solution)/shard_map/ppermute | solution.py:282
  5.4 2.0 collective-permute-start.2
  7.5 3.3 %fusion = (bf16[2304,512]{1,0:T(8,128)(2,1)S(1)}, bf16[2304,512]{1,0:T(8,128)(2,1)S(1)}) fusion(f32[2304,512]{1,0:T(8,128)} %param.7), kind=kLoop, calls=%fused_computation.8 | loop fusion | flops 4718592 | bytes 9437184 | tf_op jit(solution)/shard_map/convert_element_type | solution.py:336
  14.1 3.9 %collective-permute-start.5 = (f32[16,2304]{1,0:T(8,128)S(1)}, f32[16,2304]{1,0:T(8,128)S(1)}, u32[]{:S(2)}, u32[]{:S(2)}) collective-permute-start(f32[16,2304]{1,0:T(8,128)S(1)} %get-tuple-element.1321), channel_id=1, source_target_pairs={{0,24},{8,0},{16,8},{24,16},{1,25},{9,1},{17,9},{25,17},{2,26},{10... | collective-permute-start | bytes 442376 | tf_op jit(solution)/shard_map/ppermute | solution.py:282
  18.9 3.4 %collective-permute-done.5 = f32[16,2304]{1,0:T(8,128)S(1)} collective-permute-done((f32[16,2304]{1,0:T(8,128)S(1)}, f32[16,2304]{1,0:T(8,128)S(1)}, u32[]{:S(2)}, u32[]{:S(2)}) %collective-permute-start.5) | collective-permute-done | bytes 147488 | tf_op jit(solution)/shard_map/ppermute | solution.py:282
  23.0 2.9 %collective-permute-done.3 = f32[16,2304]{1,0:T(8,128)S(1)} collective-permute-done((f32[16,2304]{1,0:T(8,128)S(1)}, f32[16,2304]{1,0:T(8,128)S(1)}, u32[]{:S(2)}, u32[]{:S(2)}) %collective-permute-start.3) | collective-permute-done | bytes 147488 | tf_op jit(solution)/shard_map/ppermute | solution.py:282
  29.2 3.8 %collective-permute-start.13 = (f32[16,2304]{1,0:T(8,128)S(1)}, f32[16,2304]{1,0:T(8,128)S(1)}, u32[]{:S(2)}, u32[]{:S(2)}) collective-permute-start(f32[16,2304]{1,0:T(8,128)S(1)} %get-tuple-element.1332), channel_id=1, source_target_pairs={{0,24},{8,0},{16,8},{24,16},{1,25},{9,1},{17,9},{25,17},{2,26},{10... | collective-permute-start | bytes 442376 | tf_op jit(solution)/shard_map/ppermute | solution.py:282
  34.6 3.0 %collective-permute-done.10 = f32[16,2304]{1,0:T(8,128)S(1)} collective-permute-done((f32[16,2304]{1,0:T(8,128)S(1)}, f32[16,2304]{1,0:T(8,128)S(1)}, u32[]{:S(2)}, u32[]{:S(2)}) %collective-permute-start.10) | collective-permute-done | bytes 147488 | tf_op jit(solution)/shard_map/ppermute | solution.py:282
  37.7 3.8 %collective-permute-start.11 = (f32[16,2304]{1,0:T(8,128)S(1)}, f32[16,2304]{1,0:T(8,128)S(1)}, u32[]{:S(2)}, u32[]{:S(2)}) collective-permute-start(f32[16,2304]{1,0:T(8,128)S(1)} %get-tuple-element.1416), channel_id=1, source_target_pairs={{0,24},{8,0},{16,8},{24,16},{1,25},{9,1},{17,9},{25,17},{2,26},{10... | collective-permute-start | bytes 442376 | tf_op jit(solution)/shard_map/ppermute | solution.py:282
  43.2 2.6 collective-permute-done.12
  47.9 2.0 shard_map.101.refs_0_
  51.6 2.8 %collective-permute-done.16 = f32[16,2304]{1,0:T(8,128)S(1)} collective-permute-done((f32[16,2304]{1,0:T(8,128)S(1)}, f32[16,2304]{1,0:T(8,128)S(1)}, u32[]{:S(2)}, u32[]{:S(2)}) %collective-permute-start.16) | collective-permute-done | bytes 147488 | tf_op jit(solution)/shard_map/ppermute | solution.py:282
  59.5 5.3 %collective-permute-done.14.refs_1_ = f32[128,1024]{1,0:T(8,128)S(1)} collective-permute-done((f32[128,1024]{1,0:T(8,128)S(1)}, f32[128,1024]{1,0:T(8,128)S(1)}, u32[]{:S(2)}, u32[]{:S(2)}) %collective-permute-start.14) | collective-permute-done | bytes 524320 | tf_op jit(solution)/shard_map/ppermute | solution.py:269
  64.8 2.1 shard_map.103
  70.2 2.0 shard_map.104.refs_0_
  74.7 2.1 shard_map.105
  77.9 5.0 %collective-permute-done.23.second.refs_7_ = f32[64,2304]{1,0:T(8,128)S(1)} collective-permute-done((f32[64,2304]{1,0:T(8,128)S(1)}, f32[64,2304]{1,0:T(8,128)S(1)}, u32[]{:S(2)}, u32[]{:S(2)}) %collective-permute-start.23) | collective-permute-done | bytes 589856 | tf_op jit(solution)/shard_map/ppermute | solution.py:269
  82.9 2.0 shard_map.106.refs_0_
  85.9 2.1 shard_map.107
  91.7 2.6 shard_map.108
  97.9 2.3 shard_map.109
  101.7 3.2 %collective-permute-done.19 = f32[64,2304]{1,0:T(8,128)S(1)} collective-permute-done((f32[64,2304]{1,0:T(8,128)S(1)}, f32[64,2304]{1,0:T(8,128)S(1)}, u32[]{:S(2)}, u32[]{:S(2)}) %collective-permute-start.19) | collective-permute-done | bytes 589856 | tf_op jit(solution)/shard_map/ppermute | solution.py:269
  105.1 2.1 shard_map.110
  107.3 2.9 %collective-permute-start.28 = (f32[16,2304]{1,0:T(8,128)S(1)}, f32[16,2304]{1,0:T(8,128)S(1)}, u32[]{:S(2)}, u32[]{:S(2)}) collective-permute-start(f32[16,2304]{1,0:T(8,128)S(1)} %get-tuple-element.1130), channel_id=1, source_target_pairs={{0,24},{8,0},{16,8},{24,16},{1,25},{9,1},{17,9},{25,17},{2,26},{10... | collective-permute-start | bytes 442376 | tf_op jit(solution)/shard_map/ppermute | solution.py:282
  114.4 3.5 %collective-permute-done.33 = f32[16,2304]{1,0:T(8,128)S(1)} collective-permute-done((f32[16,2304]{1,0:T(8,128)S(1)}, f32[16,2304]{1,0:T(8,128)S(1)}, u32[]{:S(2)}, u32[]{:S(2)}) %collective-permute-start.33) | collective-permute-done | bytes 147488 | tf_op jit(solution)/shard_map/ppermute | solution.py:282
  118.0 2.5 collective-permute-start.34
  120.7 4.1 %collective-permute-done.34 = f32[16,2304]{1,0:T(8,128)S(1)} collective-permute-done((f32[16,2304]{1,0:T(8,128)S(1)}, f32[16,2304]{1,0:T(8,128)S(1)}, u32[]{:S(2)}, u32[]{:S(2)}) %collective-permute-start.34) | collective-permute-done | bytes 147488 | tf_op jit(solution)/shard_map/ppermute | solution.py:282
  126.5 2.2 collective-permute-start.41
  130.2 3.7 %collective-permute-start.39 = (f32[16,2304]{1,0:T(8,128)S(1)}, f32[16,2304]{1,0:T(8,128)S(1)}, u32[]{:S(2)}, u32[]{:S(2)}) collective-permute-start(f32[16,2304]{1,0:T(8,128)S(1)} %get-tuple-element.1238), channel_id=1, source_target_pairs={{0,8},{8,16},{16,24},{24,0},{1,9},{9,17},{17,25},{25,1},{2,10},{10... | collective-permute-start | bytes 442376 | tf_op jit(solution)/shard_map/ppermute | solution.py:282
  134.9 4.9 %collective-permute-start.38 = (f32[16,2304]{1,0:T(8,128)S(1)}, f32[16,2304]{1,0:T(8,128)S(1)}, u32[]{:S(2)}, u32[]{:S(2)}) collective-permute-start(f32[16,2304]{1,0:T(8,128)S(1)} %collective-permute-done.36), channel_id=1, source_target_pairs={{0,8},{8,16},{16,24},{24,0},{1,9},{9,17},{17,25},{25,1},{2,10},{10... | collective-permute-start | bytes 442376 | tf_op jit(solution)/shard_map/ppermute | solution.py:282
  142.0 2.0 collective-permute-done.38
  147.4 2.5 collective-permute-done.45
  152.2 4.4 %collective-permute-start.46 = (f32[16,2304]{1,0:T(8,128)S(1)}, f32[16,2304]{1,0:T(8,128)S(1)}, u32[]{:S(2)}, u32[]{:S(2)}) collective-permute-start(f32[16,2304]{1,0:T(8,128)S(1)} %get-tuple-element.1306), channel_id=1, source_target_pairs={{0,24},{8,0},{16,8},{24,16},{1,25},{9,1},{17,9},{25,17},{2,26},{10... | collective-permute-start | bytes 442376 | tf_op jit(solution)/shard_map/ppermute | solution.py:282
  160.7 4.6 %collective-permute-done.49 = f32[16,2304]{1,0:T(8,128)S(1)} collective-permute-done((f32[16,2304]{1,0:T(8,128)S(1)}, f32[16,2304]{1,0:T(8,128)S(1)}, u32[]{:S(2)}, u32[]{:S(2)}) %collective-permute-start.49) | collective-permute-done | bytes 147488 | tf_op jit(solution)/shard_map/ppermute | solution.py:282
  165.3 2.0 collective-permute-start.54
  167.3 3.2 %shard_map.113 = (f32[128,1024]{1,0:T(8,128)S(1)}, f32[2,8,2304]{2,1,0:T(8,128)S(1)}) custom-call(f32[64,2304]{1,0:T(8,128)S(1)} %pad_maximum_fusion.12.first.refs_0_, f32[64,2304]{1,0:T(8,128)S(1)} %collective-permute-done.42.second.refs_1_, bf16[512,2304]{1,0:T(8,128)(2,1)S(1)} %get-tuple-element.1503.refs_3_.own_high, ...), custom_call_target="tpu_custom_call" | custom-call | flops 1 | bytes 1 | tf_op jit(solution)/shard_map/pallas_call | solution.py:66
  175.8 2.6 collective-permute-start.56
  178.4 3.3 %collective-permute-done.52 = f32[16,2304]{1,0:T(8,128)S(1)} collective-permute-done((f32[16,2304]{1,0:T(8,128)S(1)}, f32[16,2304]{1,0:T(8,128)S(1)}, u32[]{:S(2)}, u32[]{:S(2)}) %collective-permute-start.52) | collective-permute-done | bytes 147488 | tf_op jit(solution)/shard_map/ppermute | solution.py:282
  185.0 3.7 %collective-permute-done.60 = f32[16,2304]{1,0:T(8,128)S(1)} collective-permute-done((f32[16,2304]{1,0:T(8,128)S(1)}, f32[16,2304]{1,0:T(8,128)S(1)}, u32[]{:S(2)}, u32[]{:S(2)}) %collective-permute-start.60) | collective-permute-done | bytes 147488 | tf_op jit(solution)/shard_map/ppermute | solution.py:282
  188.7 3.8 %collective-permute-start.58 = (f32[16,2304]{1,0:T(8,128)S(1)}, f32[16,2304]{1,0:T(8,128)S(1)}, u32[]{:S(2)}, u32[]{:S(2)}) collective-permute-start(f32[16,2304]{1,0:T(8,128)S(1)} %add_subtract_fusion), channel_id=1, source_target_pairs={{0,24},{8,0},{16,8},{24,16},{1,25},{9,1},{17,9},{25,17},{2,26},{10... | collective-permute-start | bytes 442376 | tf_op jit(solution)/shard_map/ppermute | solution.py:282
  192.6 3.2 %collective-permute-done.59 = f32[16,2304]{1,0:T(8,128)S(1)} collective-permute-done((f32[16,2304]{1,0:T(8,128)S(1)}, f32[16,2304]{1,0:T(8,128)S(1)}, u32[]{:S(2)}, u32[]{:S(2)}) %collective-permute-start.59) | collective-permute-done | bytes 147488 | tf_op jit(solution)/shard_map/ppermute | solution.py:282
  197.9 3.2 %shard_map.114 = (f32[128,1024]{1,0:T(8,128)S(1)}, f32[2,8,2304]{2,1,0:T(8,128)S(1)}) custom-call(f32[64,2304]{1,0:T(8,128)S(1)} %pad_maximum_fusion.13.first.refs_2_, f32[64,2304]{1,0:T(8,128)S(1)} %collective-permute-done.55.second.refs_3_, bf16[512,2304]{1,0:T(8,128)(2,1)S(1)} %get-tuple-element.1503.refs_3_.own_high, ...), custom_call_target="tpu_custom_call" | custom-call | flops 1 | bytes 1 | tf_op jit(solution)/shard_map/pallas_call | solution.py:66
  204.8 7.5 %collective-permute-done.61.second.refs_5_ = f32[64,2304]{1,0:T(8,128)S(1)} collective-permute-done((f32[64,2304]{1,0:T(8,128)S(1)}, f32[64,2304]{1,0:T(8,128)S(1)}, u32[]{:S(2)}, u32[]{:S(2)}) %collective-permute-start.61) | collective-permute-done | bytes 589856 | tf_op jit(solution)/shard_map/ppermute | solution.py:269
  212.3 3.2 %shard_map.115 = (f32[128,1024]{1,0:T(8,128)S(1)}, f32[2,8,2304]{2,1,0:T(8,128)S(1)}) custom-call(f32[64,2304]{1,0:T(8,128)S(1)} %pad_maximum_fusion.14.first.refs_4_, f32[64,2304]{1,0:T(8,128)S(1)} %collective-permute-done.61.second.refs_5_, bf16[512,2304]{1,0:T(8,128)(2,1)S(1)} %get-tuple-element.1503.refs_3_.own_high, ...), custom_call_target="tpu_custom_call" | custom-call | flops 1 | bytes 1 | tf_op jit(solution)/shard_map/pallas_call | solution.py:66
  219.3 5.2 %collective-permute-done.64.second.refs_7_ = f32[64,2304]{1,0:T(8,128)S(1)} collective-permute-done((f32[64,2304]{1,0:T(8,128)S(1)}, f32[64,2304]{1,0:T(8,128)S(1)}, u32[]{:S(2)}, u32[]{:S(2)}) %collective-permute-start.64) | collective-permute-done | bytes 589856 | tf_op jit(solution)/shard_map/ppermute | solution.py:269
  224.5 3.2 %shard_map.116 = (f32[128,1024]{1,0:T(8,128)S(1)}, f32[2,8,2304]{2,1,0:T(8,128)S(1)}) custom-call(f32[64,2304]{1,0:T(8,128)S(1)} %pad_maximum_fusion.15.first.refs_6_, f32[64,2304]{1,0:T(8,128)S(1)} %collective-permute-done.64.second.refs_7_, bf16[512,2304]{1,0:T(8,128)(2,1)S(1)} %get-tuple-element.1503.refs_3_.own_high, ...), custom_call_target="tpu_custom_call" | custom-call | flops 1 | bytes 1 | tf_op jit(solution)/shard_map/pallas_call | solution.py:66
  235.1 12.3 %shard_map.117 = (f32[512,2304]{1,0:T(8,128)}, f32[1,2304]{1,0:T(1,128)}) custom-call(bf16[512,512]{1,0:T(8,128)(2,1)} %copy-done.12, bf16[512,512]{1,0:T(8,128)(2,1)} %copy-done.13, bf16[512,512]{1,0:T(8,128)(2,1)} %copy-done.14, bf16[512,512]{1,0:T(8,128)(2,1)} %copy-done.15, f32[64,2304]{1,0:T(8,128)} %copy-done, f32[64,2304]{1,0:T(8,128)} %copy-done.4, ...), custom_call_target="tpu_custom_call" | custom-call | flops 1 | bytes 1 | tf_op jit(solution)/shard_map/pallas_call | solution.py:168
  251.2 12.1 %shard_map.118 = (f32[2304,512]{1,0:T(8,128)}, f32[1,512]{1,0:T(1,128)}) custom-call(bf16[2304,512]{1,0:T(8,128)(2,1)} %copy-done.8, bf16[2304,512]{1,0:T(8,128)(2,1)} %copy-done.9, bf16[2304,512]{1,0:T(8,128)(2,1)} %copy-done.10, bf16[2304,512]{1,0:T(8,128)(2,1)} %copy-done.11, f32[128,512]{1,0:T(8,128)} %get-tuple-element.1618.refs_0_, ...), custom_call_target="tpu_custom_call" | custom-call | flops 1 | bytes 1 | tf_op jit(solution)/shard_map/pallas_call | solution.py:168
  (238 shorter events, 88.8 us)
Async XLA Ops:
  1.8 16.3 %collective-permute-start.7 = (f32[2304,512]{1,0:T(8,128)}, f32[2304,512]{1,0:T(8,128)S(1)}, u32[]{:S(2)}, u32[]{:S(2)}) collective-permute-start(f32[2304,512]{1,0:T(8,128)} %param.7), channel_id=1, source_target_pairs={{0,2},{2,0},{1,3},{3,1},{4,6},{6,4},{5,7},{7,5},{8,10},{10,8},{9,1... | collective-permute-start | bytes 14155784 | tf_op jit(solution)/shard_map/ppermute | solution.py:269
  2.3 20.0 %collective-permute-start.4 = (f32[512,2304]{1,0:T(8,128)}, f32[512,2304]{1,0:T(8,128)S(1)}, u32[]{:S(2)}, u32[]{:S(2)}) collective-permute-start(f32[512,2304]{1,0:T(8,128)} %param.10), channel_id=1, source_target_pairs={{0,2},{2,0},{1,3},{3,1},{4,6},{6,4},{5,7},{7,5},{8,10},{10,8},{9,1... | collective-permute-start | bytes 14155784 | tf_op jit(solution)/shard_map/ppermute | solution.py:269
  2.4 9.7 %collective-permute-start.1 = (f32[16,2304]{1,0:T(8,128)S(1)}, f32[16,2304]{1,0:T(8,128)S(1)}, u32[]{:S(2)}, u32[]{:S(2)}) collective-permute-start(f32[16,2304]{1,0:T(8,128)S(1)} %get-tuple-element.1219), channel_id=1, source_target_pairs={{0,8},{8,16},{16,24},{24,0},{1,9},{9,17},{17,25},{25,1},{2,10},{10... | collective-permute-start | bytes 442376 | tf_op jit(solution)/shard_map/ppermute | solution.py:282
  7.5 11.5 %collective-permute-start.6 = (f32[16,2304]{1,0:T(8,128)S(1)}, f32[16,2304]{1,0:T(8,128)S(1)}, u32[]{:S(2)}, u32[]{:S(2)}) collective-permute-start(f32[16,2304]{1,0:T(8,128)S(1)} %get-tuple-element.1321), channel_id=1, source_target_pairs={{0,8},{8,16},{16,24},{24,0},{1,9},{9,17},{17,25},{25,1},{2,10},{10... | collective-permute-start | bytes 442376 | tf_op jit(solution)/shard_map/ppermute | solution.py:282
  12.1 15.5 %collective-permute-start = (f32[2,512]{1,0:T(2,128)S(1)}, f32[2,512]{1,0:T(2,128)S(1)}, u32[]{:S(2)}, u32[]{:S(2)}) collective-permute-start(f32[2,512]{1,0:T(2,128)S(1)} %pad_maximum_fusion.18), channel_id=1, source_target_pairs={{0,2},{2,0},{1,3},{3,1},{4,6},{6,4},{5,7},{7,5},{8,10},{10,8},{9,1... | collective-permute-start | bytes 12296 | tf_op jit(solution)/shard_map/ppermute | solution.py:269
  27.5 10.1 %collective-permute-start.10 = (f32[16,2304]{1,0:T(8,128)S(1)}, f32[16,2304]{1,0:T(8,128)S(1)}, u32[]{:S(2)}, u32[]{:S(2)}) collective-permute-start(f32[16,2304]{1,0:T(8,128)S(1)} %collective-permute-done.6), channel_id=1, source_target_pairs={{0,8},{8,16},{16,24},{24,0},{1,9},{9,17},{17,25},{25,1},{2,10},{10... | collective-permute-start | bytes 442376 | tf_op jit(solution)/shard_map/ppermute | solution.py:282
  27.6 20.2 %collective-permute-start.8 = (f32[64,2304]{1,0:T(8,128)S(1)}, f32[64,2304]{1,0:T(8,128)S(1)}, u32[]{:S(2)}, u32[]{:S(2)}) collective-permute-start(f32[64,2304]{1,0:T(8,128)S(1)} %pad_maximum_fusion.8.first.refs_0_), channel_id=1, source_target_pairs={{0,4},{4,0},{1,5},{5,1},{2,6},{6,2},{3,7},{7,3},{8,12},{12,8},{9,1... | collective-permute-start | bytes 1769480 | tf_op jit(solution)/shard_map/ppermute | solution.py:269
  29.2 12.3 %collective-permute-start.13 = (f32[16,2304]{1,0:T(8,128)S(1)}, f32[16,2304]{1,0:T(8,128)S(1)}, u32[]{:S(2)}, u32[]{:S(2)}) collective-permute-start(f32[16,2304]{1,0:T(8,128)S(1)} %get-tuple-element.1332), channel_id=1, source_target_pairs={{0,24},{8,0},{16,8},{24,16},{1,25},{9,1},{17,9},{25,17},{2,26},{10... | collective-permute-start | bytes 442376 | tf_op jit(solution)/shard_map/ppermute | solution.py:282
  37.7 9.5 %collective-permute-start.11 = (f32[16,2304]{1,0:T(8,128)S(1)}, f32[16,2304]{1,0:T(8,128)S(1)}, u32[]{:S(2)}, u32[]{:S(2)}) collective-permute-start(f32[16,2304]{1,0:T(8,128)S(1)} %get-tuple-element.1416), channel_id=1, source_target_pairs={{0,24},{8,0},{16,8},{24,16},{1,25},{9,1},{17,9},{25,17},{2,26},{10... | collective-permute-start | bytes 442376 | tf_op jit(solution)/shard_map/ppermute | solution.py:282
  41.6 14.4 %collective-permute-start.15 = (f32[64,2304]{1,0:T(8,128)S(1)}, f32[64,2304]{1,0:T(8,128)S(1)}, u32[]{:S(2)}, u32[]{:S(2)}) collective-permute-start(f32[64,2304]{1,0:T(8,128)S(1)} %pad_maximum_fusion.9.first.refs_2_), channel_id=1, source_target_pairs={{0,4},{4,0},{1,5},{5,1},{2,6},{6,2},{3,7},{7,3},{8,12},{12,8},{9,1... | collective-permute-start | bytes 1769480 | tf_op jit(solution)/shard_map/ppermute | solution.py:269
  49.9 14.9 %collective-permute-start.14 = (f32[128,1024]{1,0:T(8,128)S(1)}, f32[128,1024]{1,0:T(8,128)S(1)}, u32[]{:S(2)}, u32[]{:S(2)}) collective-permute-start(f32[128,1024]{1,0:T(8,128)S(1)} %shard_map.101.refs_0_), channel_id=1, source_target_pairs={{0,1},{1,0},{2,3},{3,2},{4,5},{5,4},{6,7},{7,6},{8,9},{9,8},{10,11... | collective-permute-start | bytes 1572872 | tf_op jit(solution)/shard_map/ppermute | solution.py:269
  54.4 23.5 %collective-permute-start.20 = (f32[128,2304]{1,0:T(8,128)S(1)}, f32[128,2304]{1,0:T(8,128)S(1)}, u32[]{:S(2)}, u32[]{:S(2)}) collective-permute-start(f32[128,2304]{1,0:T(8,128)S(1)} %pad_maximum_fusion), channel_id=1, source_target_pairs={{0,2},{2,0},{1,3},{3,1},{4,6},{6,4},{5,7},{7,5},{8,10},{10,8},{9,1... | collective-permute-start | bytes 3538952 | tf_op jit(solution)/shard_map/ppermute | solution.py:269
  54.4 15.8 %collective-permute-start.18 = (f32[64,2304]{1,0:T(8,128)S(1)}, f32[64,2304]{1,0:T(8,128)S(1)}, u32[]{:S(2)}, u32[]{:S(2)}) collective-permute-start(f32[64,2304]{1,0:T(8,128)S(1)} %pad_maximum_fusion.10.first.refs_4_), channel_id=1, source_target_pairs={{0,4},{4,0},{1,5},{5,1},{2,6},{6,2},{3,7},{7,3},{8,12},{12,8},{9,1... | collective-permute-start | bytes 1769480 | tf_op jit(solution)/shard_map/ppermute | solution.py:269
  58.0 16.7 %collective-permute-start.21 = (f32[128,1024]{1,0:T(8,128)S(1)}, f32[128,1024]{1,0:T(8,128)S(1)}, u32[]{:S(2)}, u32[]{:S(2)}) collective-permute-start(f32[128,1024]{1,0:T(8,128)S(1)} %shard_map.102.refs_0_), channel_id=1, source_target_pairs={{0,1},{1,0},{2,3},{3,2},{4,5},{5,4},{6,7},{7,6},{8,9},{9,8},{10,11... | collective-permute-start | bytes 1572872 | tf_op jit(solution)/shard_map/ppermute | solution.py:269
  67.1 21.1 %collective-permute-start.22 = (f32[128,2304]{1,0:T(8,128)S(1)}, f32[128,2304]{1,0:T(8,128)S(1)}, u32[]{:S(2)}, u32[]{:S(2)}) collective-permute-start(f32[128,2304]{1,0:T(8,128)S(1)} %pad_maximum_fusion.1), channel_id=1, source_target_pairs={{0,2},{2,0},{1,3},{3,1},{4,6},{6,4},{5,7},{7,5},{8,10},{10,8},{9,1... | collective-permute-start | bytes 3538952 | tf_op jit(solution)/shard_map/ppermute | solution.py:269
  67.1 15.7 %collective-permute-start.23 = (f32[64,2304]{1,0:T(8,128)S(1)}, f32[64,2304]{1,0:T(8,128)S(1)}, u32[]{:S(2)}, u32[]{:S(2)}) collective-permute-start(f32[64,2304]{1,0:T(8,128)S(1)} %pad_maximum_fusion.11.first.refs_6_), channel_id=1, source_target_pairs={{0,4},{4,0},{1,5},{5,1},{2,6},{6,2},{3,7},{7,3},{8,12},{12,8},{9,1... | collective-permute-start | bytes 1769480 | tf_op jit(solution)/shard_map/ppermute | solution.py:269
  72.2 13.7 %collective-permute-start.24 = (f32[128,1024]{1,0:T(8,128)S(1)}, f32[128,1024]{1,0:T(8,128)S(1)}, u32[]{:S(2)}, u32[]{:S(2)}) collective-permute-start(f32[128,1024]{1,0:T(8,128)S(1)} %shard_map.104.refs_0_), channel_id=1, source_target_pairs={{0,1},{1,0},{2,3},{3,2},{4,5},{5,4},{6,7},{7,6},{8,9},{9,8},{10,11... | collective-permute-start | bytes 1572872 | tf_op jit(solution)/shard_map/ppermute | solution.py:269
  74.7 13.3 %collective-permute-start.25 = (f32[128,512]{1,0:T(8,128)S(1)}, f32[128,512]{1,0:T(8,128)S(1)}, u32[]{:S(2)}, u32[]{:S(2)}) collective-permute-start(f32[128,512]{1,0:T(8,128)S(1)} %get-tuple-element.984), channel_id=1, source_target_pairs={{0,2},{2,0},{1,3},{3,1},{4,6},{6,4},{5,7},{7,5},{8,10},{10,8},{9,1... | collective-permute-start | bytes 786440 | tf_op jit(solution)/shard_map/ppermute | solution.py:269
  88.2 9.2 %collective-permute-start.27 = (f32[128,2304]{1,0:T(8,128)S(1)}, f32[128,2304]{1,0:T(8,128)S(1)}, u32[]{:S(2)}, u32[]{:S(2)}) collective-permute-start(f32[128,2304]{1,0:T(8,128)S(1)} %pad_maximum_fusion.3), channel_id=1, source_target_pairs={{0,2},{2,0},{1,3},{3,1},{4,6},{6,4},{5,7},{7,5},{8,10},{10,8},{9,1... | collective-permute-start | bytes 3538952 | tf_op jit(solution)/shard_map/ppermute | solution.py:269
  88.7 16.2 %collective-permute-start.19 = (f32[64,2304]{1,0:T(8,128)S(1)}, f32[64,2304]{1,0:T(8,128)S(1)}, u32[]{:S(2)}, u32[]{:S(2)}) collective-permute-start(f32[64,2304]{1,0:T(8,128)S(1)} %get-tuple-element.997), channel_id=1, source_target_pairs={{0,4},{4,0},{1,5},{5,1},{2,6},{6,2},{3,7},{7,3},{8,12},{12,8},{9,1... | collective-permute-start | bytes 1769480 | tf_op jit(solution)/shard_map/ppermute | solution.py:269
  90.2 20.0 %collective-permute-start.29 = (f32[128,512]{1,0:T(8,128)S(1)}, f32[128,512]{1,0:T(8,128)S(1)}, u32[]{:S(2)}, u32[]{:S(2)}) collective-permute-start(f32[128,512]{1,0:T(8,128)S(1)} %get-tuple-element.1039), channel_id=1, source_target_pairs={{0,2},{2,0},{1,3},{3,1},{4,6},{6,4},{5,7},{7,5},{8,10},{10,8},{9,1... | collective-permute-start | bytes 786440 | tf_op jit(solution)/shard_map/ppermute | solution.py:269
  90.2 14.8 %collective-permute-start.30 = (f32[128,1024]{1,0:T(8,128)S(1)}, f32[128,1024]{1,0:T(8,128)S(1)}, u32[]{:S(2)}, u32[]{:S(2)}) collective-permute-start(f32[128,1024]{1,0:T(8,128)S(1)} %shard_map.106.refs_0_), channel_id=1, source_target_pairs={{0,1},{1,0},{2,3},{3,2},{4,5},{5,4},{6,7},{7,6},{8,9},{9,8},{10,11... | collective-permute-start | bytes 1572872 | tf_op jit(solution)/shard_map/ppermute | solution.py:269
  97.2 14.4 %collective-permute-start.31 = (f32[128,512]{1,0:T(8,128)S(1)}, f32[128,512]{1,0:T(8,128)S(1)}, u32[]{:S(2)}, u32[]{:S(2)}) collective-permute-start(f32[128,512]{1,0:T(8,128)S(1)} %get-tuple-element.1113), channel_id=1, source_target_pairs={{0,2},{2,0},{1,3},{3,1},{4,6},{6,4},{5,7},{7,5},{8,10},{10,8},{9,1... | collective-permute-start | bytes 786440 | tf_op jit(solution)/shard_map/ppermute | solution.py:269
  97.4 20.5 %collective-permute-start.35 = (f32[64,2304]{1,0:T(8,128)S(1)}, f32[64,2304]{1,0:T(8,128)S(1)}, u32[]{:S(2)}, u32[]{:S(2)}) collective-permute-start(f32[64,2304]{1,0:T(8,128)S(1)} %get-tuple-element.1137), channel_id=1, source_target_pairs={{0,4},{4,0},{1,5},{5,1},{2,6},{6,2},{3,7},{7,3},{8,12},{12,8},{9,1... | collective-permute-start | bytes 1769480 | tf_op jit(solution)/shard_map/ppermute | solution.py:269
  111.5 28.2 %collective-permute-start.40 = (f32[64,2304]{1,0:T(8,128)S(1)}, f32[64,2304]{1,0:T(8,128)S(1)}, u32[]{:S(2)}, u32[]{:S(2)}) collective-permute-start(f32[64,2304]{1,0:T(8,128)S(1)} %get-tuple-element.1141), channel_id=1, source_target_pairs={{0,4},{4,0},{1,5},{5,1},{2,6},{6,2},{3,7},{7,3},{8,12},{12,8},{9,1... | collective-permute-start | bytes 1769480 | tf_op jit(solution)/shard_map/ppermute | solution.py:269
  120.6 9.6 %collective-permute-start.37 = (f32[16,2304]{1,0:T(8,128)S(1)}, f32[16,2304]{1,0:T(8,128)S(1)}, u32[]{:S(2)}, u32[]{:S(2)}) collective-permute-start(f32[16,2304]{1,0:T(8,128)S(1)} %get-tuple-element.1230), channel_id=1, source_target_pairs={{0,24},{8,0},{16,8},{24,16},{1,25},{9,1},{17,9},{25,17},{2,26},{10... | collective-permute-start | bytes 442376 | tf_op jit(solution)/shard_map/ppermute | solution.py:282
  128.7 22.6 %collective-permute-start.43 = (f32[64,2304]{1,0:T(8,128)S(1)}, f32[64,2304]{1,0:T(8,128)S(1)}, u32[]{:S(2)}, u32[]{:S(2)}) collective-permute-start(f32[64,2304]{1,0:T(8,128)S(1)} %get-tuple-element.1278), channel_id=1, source_target_pairs={{0,4},{4,0},{1,5},{5,1},{2,6},{6,2},{3,7},{7,3},{8,12},{12,8},{9,1... | collective-permute-start | bytes 1769480 | tf_op jit(solution)/shard_map/ppermute | solution.py:269
  130.2 9.7 %collective-permute-start.39 = (f32[16,2304]{1,0:T(8,128)S(1)}, f32[16,2304]{1,0:T(8,128)S(1)}, u32[]{:S(2)}, u32[]{:S(2)}) collective-permute-start(f32[16,2304]{1,0:T(8,128)S(1)} %get-tuple-element.1238), channel_id=1, source_target_pairs={{0,8},{8,16},{16,24},{24,0},{1,9},{9,17},{17,25},{25,1},{2,10},{10... | collective-permute-start | bytes 442376 | tf_op jit(solution)/shard_map/ppermute | solution.py:282
  134.9 9.2 %collective-permute-start.38 = (f32[16,2304]{1,0:T(8,128)S(1)}, f32[16,2304]{1,0:T(8,128)S(1)}, u32[]{:S(2)}, u32[]{:S(2)}) collective-permute-start(f32[16,2304]{1,0:T(8,128)S(1)} %collective-permute-done.36), channel_id=1, source_target_pairs={{0,8},{8,16},{16,24},{24,0},{1,9},{9,17},{17,25},{25,1},{2,10},{10... | collective-permute-start | bytes 442376 | tf_op jit(solution)/shard_map/ppermute | solution.py:282
  145.9 21.4 %collective-permute-start.42 = (f32[64,2304]{1,0:T(8,128)S(1)}, f32[64,2304]{1,0:T(8,128)S(1)}, u32[]{:S(2)}, u32[]{:S(2)}) collective-permute-start(f32[64,2304]{1,0:T(8,128)S(1)} %pad_maximum_fusion.12.first.refs_0_), channel_id=1, source_target_pairs={{0,4},{4,0},{1,5},{5,1},{2,6},{6,2},{3,7},{7,3},{8,12},{12,8},{9,1... | collective-permute-start | bytes 1769480 | tf_op jit(solution)/shard_map/ppermute | solution.py:269
  158.2 12.4 %collective-permute-start.50 = (f32[16,2304]{1,0:T(8,128)S(1)}, f32[16,2304]{1,0:T(8,128)S(1)}, u32[]{:S(2)}, u32[]{:S(2)}) collective-permute-start(f32[16,2304]{1,0:T(8,128)S(1)} %add_subtract_fusion.2), channel_id=1, source_target_pairs={{0,8},{8,16},{16,24},{24,0},{1,9},{9,17},{17,25},{25,1},{2,10},{10... | collective-permute-start | bytes 442376 | tf_op jit(solution)/shard_map/ppermute | solution.py:282
  165.2 9.4 %collective-permute-start.51 = (f32[16,2304]{1,0:T(8,128)S(1)}, f32[16,2304]{1,0:T(8,128)S(1)}, u32[]{:S(2)}, u32[]{:S(2)}) collective-permute-start(f32[16,2304]{1,0:T(8,128)S(1)} %add_subtract_fusion.2), channel_id=1, source_target_pairs={{0,24},{8,0},{16,8},{24,16},{1,25},{9,1},{17,9},{25,17},{2,26},{10... | collective-permute-start | bytes 442376 | tf_op jit(solution)/shard_map/ppermute | solution.py:282
  165.3 10.5 %collective-permute-start.54 = (f32[16,2304]{1,0:T(8,128)S(1)}, f32[16,2304]{1,0:T(8,128)S(1)}, u32[]{:S(2)}, u32[]{:S(2)}) collective-permute-start(f32[16,2304]{1,0:T(8,128)S(1)} %add_subtract_fusion.1), channel_id=1, source_target_pairs={{0,8},{8,16},{16,24},{24,0},{1,9},{9,17},{17,25},{25,1},{2,10},{10... | collective-permute-start | bytes 442376 | tf_op jit(solution)/shard_map/ppermute | solution.py:282
  172.4 11.0 %collective-permute-start.57 = (f32[128,1024]{1,0:T(8,128)S(1)}, f32[128,1024]{1,0:T(8,128)S(1)}, u32[]{:S(2)}, u32[]{:S(2)}) collective-permute-start(f32[128,1024]{1,0:T(8,128)S(1)} %get-tuple-element.1405), channel_id=1, source_target_pairs={{0,1},{1,0},{2,3},{3,2},{4,5},{5,4},{6,7},{7,6},{8,9},{9,8},{10,11... | collective-permute-start | bytes 1572872 | tf_op jit(solution)/shard_map/ppermute | solution.py:269
  181.8 16.1 %collective-permute-start.55 = (f32[64,2304]{1,0:T(8,128)S(1)}, f32[64,2304]{1,0:T(8,128)S(1)}, u32[]{:S(2)}, u32[]{:S(2)}) collective-permute-start(f32[64,2304]{1,0:T(8,128)S(1)} %pad_maximum_fusion.13.first.refs_2_), channel_id=1, source_target_pairs={{0,4},{4,0},{1,5},{5,1},{2,6},{6,2},{3,7},{7,3},{8,12},{12,8},{9,1... | collective-permute-start | bytes 1769480 | tf_op jit(solution)/shard_map/ppermute | solution.py:269
  196.0 23.0 %collective-permute-start.65 = (f32[128,2304]{1,0:T(8,128)S(1)}, f32[128,2304]{1,0:T(8,128)S(1)}, u32[]{:S(2)}, u32[]{:S(2)}) collective-permute-start(f32[128,2304]{1,0:T(8,128)S(1)} %pad_maximum_fusion.4), channel_id=1, source_target_pairs={{0,2},{2,0},{1,3},{3,1},{4,6},{6,4},{5,7},{7,5},{8,10},{10,8},{9,1... | collective-permute-start | bytes 3538952 | tf_op jit(solution)/shard_map/ppermute | solution.py:269
  196.1 16.2 %collective-permute-start.61 = (f32[64,2304]{1,0:T(8,128)S(1)}, f32[64,2304]{1,0:T(8,128)S(1)}, u32[]{:S(2)}, u32[]{:S(2)}) collective-permute-start(f32[64,2304]{1,0:T(8,128)S(1)} %pad_maximum_fusion.14.first.refs_4_), channel_id=1, source_target_pairs={{0,4},{4,0},{1,5},{5,1},{2,6},{6,2},{3,7},{7,3},{8,12},{12,8},{9,1... | collective-permute-start | bytes 1769480 | tf_op jit(solution)/shard_map/ppermute | solution.py:269
  197.8 31.1 %collective-permute-start.67 = (f32[128,512]{1,0:T(8,128)S(1)}, f32[128,512]{1,0:T(8,128)S(1)}, u32[]{:S(2)}, u32[]{:S(2)}) collective-permute-start(f32[128,512]{1,0:T(8,128)S(1)} %get-tuple-element.1520), channel_id=1, source_target_pairs={{0,2},{2,0},{1,3},{3,1},{4,6},{6,4},{5,7},{7,5},{8,10},{10,8},{9,1... | collective-permute-start | bytes 786440 | tf_op jit(solution)/shard_map/ppermute | solution.py:269
  201.1 14.4 %collective-permute-start.63 = (f32[128,1024]{1,0:T(8,128)S(1)}, f32[128,1024]{1,0:T(8,128)S(1)}, u32[]{:S(2)}, u32[]{:S(2)}) collective-permute-start(f32[128,1024]{1,0:T(8,128)S(1)} %get-tuple-element.1481), channel_id=1, source_target_pairs={{0,1},{1,0},{2,3},{3,2},{4,5},{5,4},{6,7},{7,6},{8,9},{9,8},{10,11... | collective-permute-start | bytes 1572872 | tf_op jit(solution)/shard_map/ppermute | solution.py:269
  203.1 21.4 %collective-permute-start.64 = (f32[64,2304]{1,0:T(8,128)S(1)}, f32[64,2304]{1,0:T(8,128)S(1)}, u32[]{:S(2)}, u32[]{:S(2)}) collective-permute-start(f32[64,2304]{1,0:T(8,128)S(1)} %pad_maximum_fusion.15.first.refs_6_), channel_id=1, source_target_pairs={{0,4},{4,0},{1,5},{5,1},{2,6},{6,2},{3,7},{7,3},{8,12},{12,8},{9,1... | collective-permute-start | bytes 1769480 | tf_op jit(solution)/shard_map/ppermute | solution.py:269
  212.3 20.9 %collective-permute-start.68 = (f32[128,2304]{1,0:T(8,128)S(1)}, f32[128,2304]{1,0:T(8,128)S(1)}, u32[]{:S(2)}, u32[]{:S(2)}) collective-permute-start(f32[128,2304]{1,0:T(8,128)S(1)} %pad_maximum_fusion.5), channel_id=1, source_target_pairs={{0,2},{2,0},{1,3},{3,1},{4,6},{6,4},{5,7},{7,5},{8,10},{10,8},{9,1... | collective-permute-start | bytes 3538952 | tf_op jit(solution)/shard_map/ppermute | solution.py:269
  216.5 14.3 %collective-permute-start.66 = (f32[128,1024]{1,0:T(8,128)S(1)}, f32[128,1024]{1,0:T(8,128)S(1)}, u32[]{:S(2)}, u32[]{:S(2)}) collective-permute-start(f32[128,1024]{1,0:T(8,128)S(1)} %get-tuple-element.1526), channel_id=1, source_target_pairs={{0,1},{1,0},{2,3},{3,2},{4,5},{5,4},{6,7},{7,6},{8,9},{9,8},{10,11... | collective-permute-start | bytes 1572872 | tf_op jit(solution)/shard_map/ppermute | solution.py:269
  219.1 15.4 %collective-permute-start.69 = (f32[128,512]{1,0:T(8,128)}, f32[128,512]{1,0:T(8,128)S(1)}, u32[]{:S(2)}, u32[]{:S(2)}) collective-permute-start(f32[128,512]{1,0:T(8,128)} %get-tuple-element.1544), channel_id=1, source_target_pairs={{0,2},{2,0},{1,3},{3,1},{4,6},{6,4},{5,7},{7,5},{8,10},{10,8},{9,1... | collective-permute-start | bytes 786440 | tf_op jit(solution)/shard_map/ppermute | solution.py:269
  224.5 10.6 %collective-permute-start.71 = (f32[128,2304]{1,0:T(8,128)}, f32[128,2304]{1,0:T(8,128)}, u32[]{:S(2)}, u32[]{:S(2)}) collective-permute-start(f32[128,2304]{1,0:T(8,128)} %pad_maximum_fusion.6), channel_id=1, source_target_pairs={{0,2},{2,0},{1,3},{3,1},{4,6},{6,4},{5,7},{7,5},{8,10},{10,8},{9,1... | collective-permute-start | bytes 3538952 | tf_op jit(solution)/shard_map/ppermute | solution.py:269
  230.8 17.3 %collective-permute-start.74 = (f32[128,1024]{1,0:T(8,128)S(1)}, f32[128,1024]{1,0:T(8,128)S(1)}, u32[]{:S(2)}, u32[]{:S(2)}) collective-permute-start(f32[128,1024]{1,0:T(8,128)S(1)} %get-tuple-element.1601), channel_id=1, source_target_pairs={{0,1},{1,0},{2,3},{3,2},{4,5},{5,4},{6,7},{7,6},{8,9},{9,8},{10,11... | collective-permute-start | bytes 1572872 | tf_op jit(solution)/shard_map/ppermute | solution.py:269
  234.5 12.9 %collective-permute-start.70 = (f32[2,2304]{1,0:T(2,128)S(1)}, f32[2,2304]{1,0:T(2,128)S(1)}, u32[]{:S(2)}, u32[]{:S(2)}) collective-permute-start(f32[2,2304]{1,0:T(2,128)S(1)} %pad_maximum_fusion.16), channel_id=1, source_target_pairs={{0,2},{2,0},{1,3},{3,1},{4,6},{6,4},{5,7},{7,5},{8,10},{10,8},{9,1... | collective-permute-start | bytes 55304 | tf_op jit(solution)/shard_map/ppermute | solution.py:269
  234.6 14.5 %collective-permute-start.75 = (f32[128,512]{1,0:T(8,128)S(1)}, f32[128,512]{1,0:T(8,128)S(1)}, u32[]{:S(2)}, u32[]{:S(2)}) collective-permute-start(f32[128,512]{1,0:T(8,128)S(1)} %get-tuple-element.1595), channel_id=1, source_target_pairs={{0,2},{2,0},{1,3},{3,1},{4,6},{6,4},{5,7},{7,5},{8,10},{10,8},{9,1... | collective-permute-start | bytes 786440 | tf_op jit(solution)/shard_map/ppermute | solution.py:269
  249.0 14.3 %collective-permute-start.73 = (f32[1]{0:T(128)}, f32[1]{0:T(128)}, u32[]{:S(2)}, u32[]{:S(2)}) collective-permute-start(f32[1]{0:T(128)} %bitcast.6), channel_id=1, source_target_pairs={{0,1},{1,0},{2,3},{3,2},{4,5},{5,4},{6,7},{7,6},{8,9},{9,8},{10,11... | collective-permute-start | bytes 20 | tf_op jit(solution)/shard_map/ppermute | solution.py:269
  (56 other events, 434.8 us)

commit v3 on v2

--- a/solution.py
+++ b/solution.py
@@ -162,9 +162,9 @@
     pieces = [*near_pieces, *far_pieces]
     columns = pieces[0].shape[1]
     if by_rows:
-        tm, tn = TILE if rows % TILE == 0 else rows, columns
+        tm, tn = TILE // 2 if rows % TILE == 0 else rows, columns
     else:
-        tm, tn = rows, TILE if columns % TILE == 0 else columns
+        tm, tn = rows, TILE // 3 if columns % TILE == 0 else columns
     return pl.pallas_call(
         functools.partial(grad_kernel, scale),
         out_shape=(

time: 270 us -> 267 us (0.989); the launches traced: 266 us -> 267 us
  transfers between devices with their start and end apart: 77 -> 77, of which waited for: 35 -> 35; matrix products, arithmetic and copies ran while one was open for 6% -> 6% of each run, Pallas kernels for 22% -> 23%
where the time goes in v3:
time: 267 us
  starting transfers between devices  92.4 us (35%)
  waiting for transfers between devices  86.8 us (33%)
  Pallas kernels  61 us (23%)
  other arithmetic  11.5 us (4%)
  local copies, waits for them, and re-layouts  11.3 us (4%)
  between operations  3.84 us (1%)
    ppermute x36, starting transfers between devices, shift(): lax.ppermute(x, 'z', [(i, (i + by) % long) for i in range(long)])  58.9 us
    ppermute x36, waiting for transfers between devices, shift(): lax.ppermute(x, 'z', [(i, (i + by) % long) for i in range(long)])  54.6 us
    ppermute x41, starting transfers between devices, swap(): return lambda x: lax.ppermute(x, axis, SWAP)  33.5 us
    ppermute x41, waiting for transfers between devices, swap(): return lambda x: lax.ppermute(x, axis, SWAP)  32.2 us
    pallas_call x2, Pallas kernels, grad(): pl.pallas_call(functools.partial(grad_kernel, scale), out_shape=(jax.Shap...  26.1 us
    pallas_call x8, Pallas kernels, product(): pl.pallas_call(functools.partial(product_kernel, dims, slots), out_shape=...  20.7 us
    pallas_call x4, Pallas kernels, gate(): pl.pallas_call(functools.partial(gate_kernel, len(parts)), out_shape=(slo...  8.47 us
    unnamed x54, local copies, waits for them, and re-layouts  6.82 us
  transfers between devices with their start and end apart: 77, of which 35 were waited for; matrix products, arithmetic and copies ran while one was open for 6% of the time, Pallas kernels for 23%

profile of v3, /device:TPU:0, one launch (start us, length us, event | category | flops | bytes accessed | tf_op | source)
XLA Modules:
  0.0 266.8 jit_solution(9533811511575945579)
XLA Ops:
  2.4 3.0 %collective-permute-start.1 = (f32[16,2304]{1,0:T(8,128)S(1)}, f32[16,2304]{1,0:T(8,128)S(1)}, u32[]{:S(2)}, u32[]{:S(2)}) collective-permute-start(f32[16,2304]{1,0:T(8,128)S(1)} %get-tuple-element.1219), channel_id=1, source_target_pairs={{0,8},{8,16},{16,24},{24,0},{1,9},{9,17},{17,25},{25,1},{2,10},{10... | collective-permute-start | bytes 442376 | tf_op jit(solution)/shard_map/ppermute | solution.py:282
  5.4 2.0 collective-permute-start.2
  7.5 3.3 %fusion = (bf16[2304,512]{1,0:T(8,128)(2,1)S(1)}, bf16[2304,512]{1,0:T(8,128)(2,1)S(1)}) fusion(f32[2304,512]{1,0:T(8,128)} %param.7), kind=kLoop, calls=%fused_computation.8 | loop fusion | flops 4718592 | bytes 9437184 | tf_op jit(solution)/shard_map/convert_element_type | solution.py:336
  14.1 3.9 %collective-permute-start.5 = (f32[16,2304]{1,0:T(8,128)S(1)}, f32[16,2304]{1,0:T(8,128)S(1)}, u32[]{:S(2)}, u32[]{:S(2)}) collective-permute-start(f32[16,2304]{1,0:T(8,128)S(1)} %get-tuple-element.1321), channel_id=1, source_target_pairs={{0,24},{8,0},{16,8},{24,16},{1,25},{9,1},{17,9},{25,17},{2,26},{10... | collective-permute-start | bytes 442376 | tf_op jit(solution)/shard_map/ppermute | solution.py:282
  18.9 3.4 %collective-permute-done.5 = f32[16,2304]{1,0:T(8,128)S(1)} collective-permute-done((f32[16,2304]{1,0:T(8,128)S(1)}, f32[16,2304]{1,0:T(8,128)S(1)}, u32[]{:S(2)}, u32[]{:S(2)}) %collective-permute-start.5) | collective-permute-done | bytes 147488 | tf_op jit(solution)/shard_map/ppermute | solution.py:282
  23.0 2.9 %collective-permute-done.3 = f32[16,2304]{1,0:T(8,128)S(1)} collective-permute-done((f32[16,2304]{1,0:T(8,128)S(1)}, f32[16,2304]{1,0:T(8,128)S(1)}, u32[]{:S(2)}, u32[]{:S(2)}) %collective-permute-start.3) | collective-permute-done | bytes 147488 | tf_op jit(solution)/shard_map/ppermute | solution.py:282
  29.2 3.8 %collective-permute-start.13 = (f32[16,2304]{1,0:T(8,128)S(1)}, f32[16,2304]{1,0:T(8,128)S(1)}, u32[]{:S(2)}, u32[]{:S(2)}) collective-permute-start(f32[16,2304]{1,0:T(8,128)S(1)} %get-tuple-element.1332), channel_id=1, source_target_pairs={{0,24},{8,0},{16,8},{24,16},{1,25},{9,1},{17,9},{25,17},{2,26},{10... | collective-permute-start | bytes 442376 | tf_op jit(solution)/shard_map/ppermute | solution.py:282
  34.6 3.0 %collective-permute-done.10 = f32[16,2304]{1,0:T(8,128)S(1)} collective-permute-done((f32[16,2304]{1,0:T(8,128)S(1)}, f32[16,2304]{1,0:T(8,128)S(1)}, u32[]{:S(2)}, u32[]{:S(2)}) %collective-permute-start.10) | collective-permute-done | bytes 147488 | tf_op jit(solution)/shard_map/ppermute | solution.py:282
  37.7 3.8 %collective-permute-start.11 = (f32[16,2304]{1,0:T(8,128)S(1)}, f32[16,2304]{1,0:T(8,128)S(1)}, u32[]{:S(2)}, u32[]{:S(2)}) collective-permute-start(f32[16,2304]{1,0:T(8,128)S(1)} %get-tuple-element.1416), channel_id=1, source_target_pairs={{0,24},{8,0},{16,8},{24,16},{1,25},{9,1},{17,9},{25,17},{2,26},{10... | collective-permute-start | bytes 442376 | tf_op jit(solution)/shard_map/ppermute | solution.py:282
  43.2 2.6 collective-permute-done.12
  47.7 2.0 shard_map.101.refs_0_
  51.4 2.8 %collective-permute-done.16 = f32[16,2304]{1,0:T(8,128)S(1)} collective-permute-done((f32[16,2304]{1,0:T(8,128)S(1)}, f32[16,2304]{1,0:T(8,128)S(1)}, u32[]{:S(2)}, u32[]{:S(2)}) %collective-permute-start.16) | collective-permute-done | bytes 147488 | tf_op jit(solution)/shard_map/ppermute | solution.py:282
  59.4 5.3 %collective-permute-done.14.refs_1_ = f32[128,1024]{1,0:T(8,128)S(1)} collective-permute-done((f32[128,1024]{1,0:T(8,128)S(1)}, f32[128,1024]{1,0:T(8,128)S(1)}, u32[]{:S(2)}, u32[]{:S(2)}) %collective-permute-start.14) | collective-permute-done | bytes 524320 | tf_op jit(solution)/shard_map/ppermute | solution.py:269
  64.7 2.1 shard_map.103
  70.1 2.0 shard_map.104.refs_0_
  74.5 2.1 shard_map.105
  77.8 5.0 %collective-permute-done.23.second.refs_7_ = f32[64,2304]{1,0:T(8,128)S(1)} collective-permute-done((f32[64,2304]{1,0:T(8,128)S(1)}, f32[64,2304]{1,0:T(8,128)S(1)}, u32[]{:S(2)}, u32[]{:S(2)}) %collective-permute-start.23) | collective-permute-done | bytes 589856 | tf_op jit(solution)/shard_map/ppermute | solution.py:269
  82.7 2.0 shard_map.106.refs_0_
  85.8 2.1 shard_map.107
  91.6 2.4 shard_map.108
  97.6 2.3 shard_map.109
  101.3 3.4 %collective-permute-done.19 = f32[64,2304]{1,0:T(8,128)S(1)} collective-permute-done((f32[64,2304]{1,0:T(8,128)S(1)}, f32[64,2304]{1,0:T(8,128)S(1)}, u32[]{:S(2)}, u32[]{:S(2)}) %collective-permute-start.19) | collective-permute-done | bytes 589856 | tf_op jit(solution)/shard_map/ppermute | solution.py:269
  104.9 2.1 shard_map.110
  107.1 2.9 %collective-permute-start.28 = (f32[16,2304]{1,0:T(8,128)S(1)}, f32[16,2304]{1,0:T(8,128)S(1)}, u32[]{:S(2)}, u32[]{:S(2)}) collective-permute-start(f32[16,2304]{1,0:T(8,128)S(1)} %get-tuple-element.1130), channel_id=1, source_target_pairs={{0,24},{8,0},{16,8},{24,16},{1,25},{9,1},{17,9},{25,17},{2,26},{10... | collective-permute-start | bytes 442376 | tf_op jit(solution)/shard_map/ppermute | solution.py:282
  114.3 3.5 %collective-permute-done.33 = f32[16,2304]{1,0:T(8,128)S(1)} collective-permute-done((f32[16,2304]{1,0:T(8,128)S(1)}, f32[16,2304]{1,0:T(8,128)S(1)}, u32[]{:S(2)}, u32[]{:S(2)}) %collective-permute-start.33) | collective-permute-done | bytes 147488 | tf_op jit(solution)/shard_map/ppermute | solution.py:282
  117.8 2.5 collective-permute-start.34
  120.5 4.1 %collective-permute-done.34 = f32[16,2304]{1,0:T(8,128)S(1)} collective-permute-done((f32[16,2304]{1,0:T(8,128)S(1)}, f32[16,2304]{1,0:T(8,128)S(1)}, u32[]{:S(2)}, u32[]{:S(2)}) %collective-permute-start.34) | collective-permute-done | bytes 147488 | tf_op jit(solution)/shard_map/ppermute | solution.py:282
  126.4 2.2 collective-permute-start.41
  130.1 3.7 %collective-permute-start.39 = (f32[16,2304]{1,0:T(8,128)S(1)}, f32[16,2304]{1,0:T(8,128)S(1)}, u32[]{:S(2)}, u32[]{:S(2)}) collective-permute-start(f32[16,2304]{1,0:T(8,128)S(1)} %get-tuple-element.1238), channel_id=1, source_target_pairs={{0,8},{8,16},{16,24},{24,0},{1,9},{9,17},{17,25},{25,1},{2,10},{10... | collective-permute-start | bytes 442376 | tf_op jit(solution)/shard_map/ppermute | solution.py:282
  134.7 4.9 %collective-permute-start.38 = (f32[16,2304]{1,0:T(8,128)S(1)}, f32[16,2304]{1,0:T(8,128)S(1)}, u32[]{:S(2)}, u32[]{:S(2)}) collective-permute-start(f32[16,2304]{1,0:T(8,128)S(1)} %collective-permute-done.36), channel_id=1, source_target_pairs={{0,8},{8,16},{16,24},{24,0},{1,9},{9,17},{17,25},{25,1},{2,10},{10... | collective-permute-start | bytes 442376 | tf_op jit(solution)/shard_map/ppermute | solution.py:282
  141.9 2.0 collective-permute-done.38
  147.2 2.5 collective-permute-done.45
  152.1 4.4 %collective-permute-start.46 = (f32[16,2304]{1,0:T(8,128)S(1)}, f32[16,2304]{1,0:T(8,128)S(1)}, u32[]{:S(2)}, u32[]{:S(2)}) collective-permute-start(f32[16,2304]{1,0:T(8,128)S(1)} %get-tuple-element.1306), channel_id=1, source_target_pairs={{0,24},{8,0},{16,8},{24,16},{1,25},{9,1},{17,9},{25,17},{2,26},{10... | collective-permute-start | bytes 442376 | tf_op jit(solution)/shard_map/ppermute | solution.py:282
  160.5 4.6 %collective-permute-done.49 = f32[16,2304]{1,0:T(8,128)S(1)} collective-permute-done((f32[16,2304]{1,0:T(8,128)S(1)}, f32[16,2304]{1,0:T(8,128)S(1)}, u32[]{:S(2)}, u32[]{:S(2)}) %collective-permute-start.49) | collective-permute-done | bytes 147488 | tf_op jit(solution)/shard_map/ppermute | solution.py:282
  165.2 2.0 collective-permute-start.54
  167.2 3.2 %shard_map.113 = (f32[128,1024]{1,0:T(8,128)S(1)}, f32[2,8,2304]{2,1,0:T(8,128)S(1)}) custom-call(f32[64,2304]{1,0:T(8,128)S(1)} %pad_maximum_fusion.12.first.refs_0_, f32[64,2304]{1,0:T(8,128)S(1)} %collective-permute-done.42.second.refs_1_, bf16[512,2304]{1,0:T(8,128)(2,1)S(1)} %get-tuple-element.1503.refs_3_.own_high, ...), custom_call_target="tpu_custom_call" | custom-call | flops 1 | bytes 1 | tf_op jit(solution)/shard_map/pallas_call | solution.py:66
  175.7 2.6 collective-permute-start.56
  178.3 3.3 %collective-permute-done.52 = f32[16,2304]{1,0:T(8,128)S(1)} collective-permute-done((f32[16,2304]{1,0:T(8,128)S(1)}, f32[16,2304]{1,0:T(8,128)S(1)}, u32[]{:S(2)}, u32[]{:S(2)}) %collective-permute-start.52) | collective-permute-done | bytes 147488 | tf_op jit(solution)/shard_map/ppermute | solution.py:282
  184.8 3.8 %collective-permute-done.60 = f32[16,2304]{1,0:T(8,128)S(1)} collective-permute-done((f32[16,2304]{1,0:T(8,128)S(1)}, f32[16,2304]{1,0:T(8,128)S(1)}, u32[]{:S(2)}, u32[]{:S(2)}) %collective-permute-start.60) | collective-permute-done | bytes 147488 | tf_op jit(solution)/shard_map/ppermute | solution.py:282
  188.6 3.8 %collective-permute-start.58 = (f32[16,2304]{1,0:T(8,128)S(1)}, f32[16,2304]{1,0:T(8,128)S(1)}, u32[]{:S(2)}, u32[]{:S(2)}) collective-permute-start(f32[16,2304]{1,0:T(8,128)S(1)} %add_subtract_fusion), channel_id=1, source_target_pairs={{0,24},{8,0},{16,8},{24,16},{1,25},{9,1},{17,9},{25,17},{2,26},{10... | collective-permute-start | bytes 442376 | tf_op jit(solution)/shard_map/ppermute | solution.py:282
  192.5 3.2 %collective-permute-done.59 = f32[16,2304]{1,0:T(8,128)S(1)} collective-permute-done((f32[16,2304]{1,0:T(8,128)S(1)}, f32[16,2304]{1,0:T(8,128)S(1)}, u32[]{:S(2)}, u32[]{:S(2)}) %collective-permute-start.59) | collective-permute-done | bytes 147488 | tf_op jit(solution)/shard_map/ppermute | solution.py:282
  197.4 3.2 %shard_map.114 = (f32[128,1024]{1,0:T(8,128)S(1)}, f32[2,8,2304]{2,1,0:T(8,128)S(1)}) custom-call(f32[64,2304]{1,0:T(8,128)S(1)} %pad_maximum_fusion.13.first.refs_2_, f32[64,2304]{1,0:T(8,128)S(1)} %collective-permute-done.55.second.refs_3_, bf16[512,2304]{1,0:T(8,128)(2,1)S(1)} %get-tuple-element.1503.refs_3_.own_high, ...), custom_call_target="tpu_custom_call" | custom-call | flops 1 | bytes 1 | tf_op jit(solution)/shard_map/pallas_call | solution.py:66
  204.4 7.4 %collective-permute-done.61.second.refs_5_ = f32[64,2304]{1,0:T(8,128)S(1)} collective-permute-done((f32[64,2304]{1,0:T(8,128)S(1)}, f32[64,2304]{1,0:T(8,128)S(1)}, u32[]{:S(2)}, u32[]{:S(2)}) %collective-permute-start.61) | collective-permute-done | bytes 589856 | tf_op jit(solution)/shard_map/ppermute | solution.py:269
  211.8 3.2 %shard_map.115 = (f32[128,1024]{1,0:T(8,128)S(1)}, f32[2,8,2304]{2,1,0:T(8,128)S(1)}) custom-call(f32[64,2304]{1,0:T(8,128)S(1)} %pad_maximum_fusion.14.first.refs_4_, f32[64,2304]{1,0:T(8,128)S(1)} %collective-permute-done.61.second.refs_5_, bf16[512,2304]{1,0:T(8,128)(2,1)S(1)} %get-tuple-element.1503.refs_3_.own_high, ...), custom_call_target="tpu_custom_call" | custom-call | flops 1 | bytes 1 | tf_op jit(solution)/shard_map/pallas_call | solution.py:66
  218.8 5.3 %collective-permute-done.64.second.refs_7_ = f32[64,2304]{1,0:T(8,128)S(1)} collective-permute-done((f32[64,2304]{1,0:T(8,128)S(1)}, f32[64,2304]{1,0:T(8,128)S(1)}, u32[]{:S(2)}, u32[]{:S(2)}) %collective-permute-start.64) | collective-permute-done | bytes 589856 | tf_op jit(solution)/shard_map/ppermute | solution.py:269
  224.1 3.2 %shard_map.116 = (f32[128,1024]{1,0:T(8,128)S(1)}, f32[2,8,2304]{2,1,0:T(8,128)S(1)}) custom-call(f32[64,2304]{1,0:T(8,128)S(1)} %pad_maximum_fusion.15.first.refs_6_, f32[64,2304]{1,0:T(8,128)S(1)} %collective-permute-done.64.second.refs_7_, bf16[512,2304]{1,0:T(8,128)(2,1)S(1)} %get-tuple-element.1503.refs_3_.own_high, ...), custom_call_target="tpu_custom_call" | custom-call | flops 1 | bytes 1 | tf_op jit(solution)/shard_map/pallas_call | solution.py:66
  234.5 13.7 %shard_map.117 = (f32[512,2304]{1,0:T(8,128)}, f32[1,2304]{1,0:T(1,128)}) custom-call(bf16[512,512]{1,0:T(8,128)(2,1)} %copy-done.12, bf16[512,512]{1,0:T(8,128)(2,1)} %copy-done.13, bf16[512,512]{1,0:T(8,128)(2,1)} %copy-done.14, bf16[512,512]{1,0:T(8,128)(2,1)} %copy-done.15, f32[64,2304]{1,0:T(8,128)} %copy-done, f32[64,2304]{1,0:T(8,128)} %copy-done.4, ...), custom_call_target="tpu_custom_call" | custom-call | flops 1 | bytes 1 | tf_op jit(solution)/shard_map/pallas_call | solution.py:168
  252.0 12.4 %shard_map.118 = (f32[2304,512]{1,0:T(8,128)}, f32[1,512]{1,0:T(1,128)}) custom-call(bf16[2304,512]{1,0:T(8,128)(2,1)} %copy-done.8, bf16[2304,512]{1,0:T(8,128)(2,1)} %copy-done.9, bf16[2304,512]{1,0:T(8,128)(2,1)} %copy-done.10, bf16[2304,512]{1,0:T(8,128)(2,1)} %copy-done.11, f32[128,512]{1,0:T(8,128)} %get-tuple-element.1618.refs_0_, ...), custom_call_target="tpu_custom_call" | custom-call | flops 1 | bytes 1 | tf_op jit(solution)/shard_map/pallas_call | solution.py:168
  (238 shorter events, 88.2 us)
Async XLA Ops:
  1.8 16.3 %collective-permute-start.7 = (f32[2304,512]{1,0:T(8,128)}, f32[2304,512]{1,0:T(8,128)S(1)}, u32[]{:S(2)}, u32[]{:S(2)}) collective-permute-start(f32[2304,512]{1,0:T(8,128)} %param.7), channel_id=1, source_target_pairs={{0,2},{2,0},{1,3},{3,1},{4,6},{6,4},{5,7},{7,5},{8,10},{10,8},{9,1... | collective-permute-start | bytes 14155784 | tf_op jit(solution)/shard_map/ppermute | solution.py:269
  2.3 20.0 %collective-permute-start.4 = (f32[512,2304]{1,0:T(8,128)}, f32[512,2304]{1,0:T(8,128)S(1)}, u32[]{:S(2)}, u32[]{:S(2)}) collective-permute-start(f32[512,2304]{1,0:T(8,128)} %param.10), channel_id=1, source_target_pairs={{0,2},{2,0},{1,3},{3,1},{4,6},{6,4},{5,7},{7,5},{8,10},{10,8},{9,1... | collective-permute-start | bytes 14155784 | tf_op jit(solution)/shard_map/ppermute | solution.py:269
  2.4 9.7 %collective-permute-start.1 = (f32[16,2304]{1,0:T(8,128)S(1)}, f32[16,2304]{1,0:T(8,128)S(1)}, u32[]{:S(2)}, u32[]{:S(2)}) collective-permute-start(f32[16,2304]{1,0:T(8,128)S(1)} %get-tuple-element.1219), channel_id=1, source_target_pairs={{0,8},{8,16},{16,24},{24,0},{1,9},{9,17},{17,25},{25,1},{2,10},{10... | collective-permute-start | bytes 442376 | tf_op jit(solution)/shard_map/ppermute | solution.py:282
  7.5 11.5 %collective-permute-start.6 = (f32[16,2304]{1,0:T(8,128)S(1)}, f32[16,2304]{1,0:T(8,128)S(1)}, u32[]{:S(2)}, u32[]{:S(2)}) collective-permute-start(f32[16,2304]{1,0:T(8,128)S(1)} %get-tuple-element.1321), channel_id=1, source_target_pairs={{0,8},{8,16},{16,24},{24,0},{1,9},{9,17},{17,25},{25,1},{2,10},{10... | collective-permute-start | bytes 442376 | tf_op jit(solution)/shard_map/ppermute | solution.py:282
  12.1 15.5 %collective-permute-start = (f32[2,512]{1,0:T(2,128)S(1)}, f32[2,512]{1,0:T(2,128)S(1)}, u32[]{:S(2)}, u32[]{:S(2)}) collective-permute-start(f32[2,512]{1,0:T(2,128)S(1)} %pad_maximum_fusion.18), channel_id=1, source_target_pairs={{0,2},{2,0},{1,3},{3,1},{4,6},{6,4},{5,7},{7,5},{8,10},{10,8},{9,1... | collective-permute-start | bytes 12296 | tf_op jit(solution)/shard_map/ppermute | solution.py:269
  27.5 10.1 %collective-permute-start.10 = (f32[16,2304]{1,0:T(8,128)S(1)}, f32[16,2304]{1,0:T(8,128)S(1)}, u32[]{:S(2)}, u32[]{:S(2)}) collective-permute-start(f32[16,2304]{1,0:T(8,128)S(1)} %collective-permute-done.6), channel_id=1, source_target_pairs={{0,8},{8,16},{16,24},{24,0},{1,9},{9,17},{17,25},{25,1},{2,10},{10... | collective-permute-start | bytes 442376 | tf_op jit(solution)/shard_map/ppermute | solution.py:282
  27.6 20.1 %collective-permute-start.8 = (f32[64,2304]{1,0:T(8,128)S(1)}, f32[64,2304]{1,0:T(8,128)S(1)}, u32[]{:S(2)}, u32[]{:S(2)}) collective-permute-start(f32[64,2304]{1,0:T(8,128)S(1)} %pad_maximum_fusion.8.first.refs_0_), channel_id=1, source_target_pairs={{0,4},{4,0},{1,5},{5,1},{2,6},{6,2},{3,7},{7,3},{8,12},{12,8},{9,1... | collective-permute-start | bytes 1769480 | tf_op jit(solution)/shard_map/ppermute | solution.py:269
  29.2 12.3 %collective-permute-start.13 = (f32[16,2304]{1,0:T(8,128)S(1)}, f32[16,2304]{1,0:T(8,128)S(1)}, u32[]{:S(2)}, u32[]{:S(2)}) collective-permute-start(f32[16,2304]{1,0:T(8,128)S(1)} %get-tuple-element.1332), channel_id=1, source_target_pairs={{0,24},{8,0},{16,8},{24,16},{1,25},{9,1},{17,9},{25,17},{2,26},{10... | collective-permute-start | bytes 442376 | tf_op jit(solution)/shard_map/ppermute | solution.py:282
  37.7 9.5 %collective-permute-start.11 = (f32[16,2304]{1,0:T(8,128)S(1)}, f32[16,2304]{1,0:T(8,128)S(1)}, u32[]{:S(2)}, u32[]{:S(2)}) collective-permute-start(f32[16,2304]{1,0:T(8,128)S(1)} %get-tuple-element.1416), channel_id=1, source_target_pairs={{0,24},{8,0},{16,8},{24,16},{1,25},{9,1},{17,9},{25,17},{2,26},{10... | collective-permute-start | bytes 442376 | tf_op jit(solution)/shard_map/ppermute | solution.py:282
  41.6 14.2 %collective-permute-start.15 = (f32[64,2304]{1,0:T(8,128)S(1)}, f32[64,2304]{1,0:T(8,128)S(1)}, u32[]{:S(2)}, u32[]{:S(2)}) collective-permute-start(f32[64,2304]{1,0:T(8,128)S(1)} %pad_maximum_fusion.9.first.refs_2_), channel_id=1, source_target_pairs={{0,4},{4,0},{1,5},{5,1},{2,6},{6,2},{3,7},{7,3},{8,12},{12,8},{9,1... | collective-permute-start | bytes 1769480 | tf_op jit(solution)/shard_map/ppermute | solution.py:269
  49.8 14.9 %collective-permute-start.14 = (f32[128,1024]{1,0:T(8,128)S(1)}, f32[128,1024]{1,0:T(8,128)S(1)}, u32[]{:S(2)}, u32[]{:S(2)}) collective-permute-start(f32[128,1024]{1,0:T(8,128)S(1)} %shard_map.101.refs_0_), channel_id=1, source_target_pairs={{0,1},{1,0},{2,3},{3,2},{4,5},{5,4},{6,7},{7,6},{8,9},{9,8},{10,11... | collective-permute-start | bytes 1572872 | tf_op jit(solution)/shard_map/ppermute | solution.py:269
  54.2 23.5 %collective-permute-start.20 = (f32[128,2304]{1,0:T(8,128)S(1)}, f32[128,2304]{1,0:T(8,128)S(1)}, u32[]{:S(2)}, u32[]{:S(2)}) collective-permute-start(f32[128,2304]{1,0:T(8,128)S(1)} %pad_maximum_fusion), channel_id=1, source_target_pairs={{0,2},{2,0},{1,3},{3,1},{4,6},{6,4},{5,7},{7,5},{8,10},{10,8},{9,1... | collective-permute-start | bytes 3538952 | tf_op jit(solution)/shard_map/ppermute | solution.py:269
  54.3 15.8 %collective-permute-start.18 = (f32[64,2304]{1,0:T(8,128)S(1)}, f32[64,2304]{1,0:T(8,128)S(1)}, u32[]{:S(2)}, u32[]{:S(2)}) collective-permute-start(f32[64,2304]{1,0:T(8,128)S(1)} %pad_maximum_fusion.10.first.refs_4_), channel_id=1, source_target_pairs={{0,4},{4,0},{1,5},{5,1},{2,6},{6,2},{3,7},{7,3},{8,12},{12,8},{9,1... | collective-permute-start | bytes 1769480 | tf_op jit(solution)/shard_map/ppermute | solution.py:269
  57.8 16.7 %collective-permute-start.21 = (f32[128,1024]{1,0:T(8,128)S(1)}, f32[128,1024]{1,0:T(8,128)S(1)}, u32[]{:S(2)}, u32[]{:S(2)}) collective-permute-start(f32[128,1024]{1,0:T(8,128)S(1)} %shard_map.102.refs_0_), channel_id=1, source_target_pairs={{0,1},{1,0},{2,3},{3,2},{4,5},{5,4},{6,7},{7,6},{8,9},{9,8},{10,11... | collective-permute-start | bytes 1572872 | tf_op jit(solution)/shard_map/ppermute | solution.py:269
  66.9 21.1 %collective-permute-start.22 = (f32[128,2304]{1,0:T(8,128)S(1)}, f32[128,2304]{1,0:T(8,128)S(1)}, u32[]{:S(2)}, u32[]{:S(2)}) collective-permute-start(f32[128,2304]{1,0:T(8,128)S(1)} %pad_maximum_fusion.1), channel_id=1, source_target_pairs={{0,2},{2,0},{1,3},{3,1},{4,6},{6,4},{5,7},{7,5},{8,10},{10,8},{9,1... | collective-permute-start | bytes 3538952 | tf_op jit(solution)/shard_map/ppermute | solution.py:269
  67.0 15.7 %collective-permute-start.23 = (f32[64,2304]{1,0:T(8,128)S(1)}, f32[64,2304]{1,0:T(8,128)S(1)}, u32[]{:S(2)}, u32[]{:S(2)}) collective-permute-start(f32[64,2304]{1,0:T(8,128)S(1)} %pad_maximum_fusion.11.first.refs_6_), channel_id=1, source_target_pairs={{0,4},{4,0},{1,5},{5,1},{2,6},{6,2},{3,7},{7,3},{8,12},{12,8},{9,1... | collective-permute-start | bytes 1769480 | tf_op jit(solution)/shard_map/ppermute | solution.py:269
  72.1 13.7 %collective-permute-start.24 = (f32[128,1024]{1,0:T(8,128)S(1)}, f32[128,1024]{1,0:T(8,128)S(1)}, u32[]{:S(2)}, u32[]{:S(2)}) collective-permute-start(f32[128,1024]{1,0:T(8,128)S(1)} %shard_map.104.refs_0_), channel_id=1, source_target_pairs={{0,1},{1,0},{2,3},{3,2},{4,5},{5,4},{6,7},{7,6},{8,9},{9,8},{10,11... | collective-permute-start | bytes 1572872 | tf_op jit(solution)/shard_map/ppermute | solution.py:269
  74.5 13.3 %collective-permute-start.25 = (f32[128,512]{1,0:T(8,128)S(1)}, f32[128,512]{1,0:T(8,128)S(1)}, u32[]{:S(2)}, u32[]{:S(2)}) collective-permute-start(f32[128,512]{1,0:T(8,128)S(1)} %get-tuple-element.984), channel_id=1, source_target_pairs={{0,2},{2,0},{1,3},{3,1},{4,6},{6,4},{5,7},{7,5},{8,10},{10,8},{9,1... | collective-permute-start | bytes 786440 | tf_op jit(solution)/shard_map/ppermute | solution.py:269
  88.5 16.2 %collective-permute-start.19 = (f32[64,2304]{1,0:T(8,128)S(1)}, f32[64,2304]{1,0:T(8,128)S(1)}, u32[]{:S(2)}, u32[]{:S(2)}) collective-permute-start(f32[64,2304]{1,0:T(8,128)S(1)} %get-tuple-element.997), channel_id=1, source_target_pairs={{0,4},{4,0},{1,5},{5,1},{2,6},{6,2},{3,7},{7,3},{8,12},{12,8},{9,1... | collective-permute-start | bytes 1769480 | tf_op jit(solution)/shard_map/ppermute | solution.py:269
  90.1 20.0 %collective-permute-start.29 = (f32[128,512]{1,0:T(8,128)S(1)}, f32[128,512]{1,0:T(8,128)S(1)}, u32[]{:S(2)}, u32[]{:S(2)}) collective-permute-start(f32[128,512]{1,0:T(8,128)S(1)} %get-tuple-element.1039), channel_id=1, source_target_pairs={{0,2},{2,0},{1,3},{3,1},{4,6},{6,4},{5,7},{7,5},{8,10},{10,8},{9,1... | collective-permute-start | bytes 786440 | tf_op jit(solution)/shard_map/ppermute | solution.py:269
  90.1 14.8 %collective-permute-start.30 = (f32[128,1024]{1,0:T(8,128)S(1)}, f32[128,1024]{1,0:T(8,128)S(1)}, u32[]{:S(2)}, u32[]{:S(2)}) collective-permute-start(f32[128,1024]{1,0:T(8,128)S(1)} %shard_map.106.refs_0_), channel_id=1, source_target_pairs={{0,1},{1,0},{2,3},{3,2},{4,5},{5,4},{6,7},{7,6},{8,9},{9,8},{10,11... | collective-permute-start | bytes 1572872 | tf_op jit(solution)/shard_map/ppermute | solution.py:269
  96.8 14.6 %collective-permute-start.31 = (f32[128,512]{1,0:T(8,128)S(1)}, f32[128,512]{1,0:T(8,128)S(1)}, u32[]{:S(2)}, u32[]{:S(2)}) collective-permute-start(f32[128,512]{1,0:T(8,128)S(1)} %get-tuple-element.1113), channel_id=1, source_target_pairs={{0,2},{2,0},{1,3},{3,1},{4,6},{6,4},{5,7},{7,5},{8,10},{10,8},{9,1... | collective-permute-start | bytes 786440 | tf_op jit(solution)/shard_map/ppermute | solution.py:269
  97.1 20.7 %collective-permute-start.35 = (f32[64,2304]{1,0:T(8,128)S(1)}, f32[64,2304]{1,0:T(8,128)S(1)}, u32[]{:S(2)}, u32[]{:S(2)}) collective-permute-start(f32[64,2304]{1,0:T(8,128)S(1)} %get-tuple-element.1137), channel_id=1, source_target_pairs={{0,4},{4,0},{1,5},{5,1},{2,6},{6,2},{3,7},{7,3},{8,12},{12,8},{9,1... | collective-permute-start | bytes 1769480 | tf_op jit(solution)/shard_map/ppermute | solution.py:269
  111.4 28.2 %collective-permute-start.40 = (f32[64,2304]{1,0:T(8,128)S(1)}, f32[64,2304]{1,0:T(8,128)S(1)}, u32[]{:S(2)}, u32[]{:S(2)}) collective-permute-start(f32[64,2304]{1,0:T(8,128)S(1)} %get-tuple-element.1141), channel_id=1, source_target_pairs={{0,4},{4,0},{1,5},{5,1},{2,6},{6,2},{3,7},{7,3},{8,12},{12,8},{9,1... | collective-permute-start | bytes 1769480 | tf_op jit(solution)/shard_map/ppermute | solution.py:269
  120.4 9.6 %collective-permute-start.37 = (f32[16,2304]{1,0:T(8,128)S(1)}, f32[16,2304]{1,0:T(8,128)S(1)}, u32[]{:S(2)}, u32[]{:S(2)}) collective-permute-start(f32[16,2304]{1,0:T(8,128)S(1)} %get-tuple-element.1230), channel_id=1, source_target_pairs={{0,24},{8,0},{16,8},{24,16},{1,25},{9,1},{17,9},{25,17},{2,26},{10... | collective-permute-start | bytes 442376 | tf_op jit(solution)/shard_map/ppermute | solution.py:282
  128.6 22.6 %collective-permute-start.43 = (f32[64,2304]{1,0:T(8,128)S(1)}, f32[64,2304]{1,0:T(8,128)S(1)}, u32[]{:S(2)}, u32[]{:S(2)}) collective-permute-start(f32[64,2304]{1,0:T(8,128)S(1)} %get-tuple-element.1278), channel_id=1, source_target_pairs={{0,4},{4,0},{1,5},{5,1},{2,6},{6,2},{3,7},{7,3},{8,12},{12,8},{9,1... | collective-permute-start | bytes 1769480 | tf_op jit(solution)/shard_map/ppermute | solution.py:269
  130.1 9.7 %collective-permute-start.39 = (f32[16,2304]{1,0:T(8,128)S(1)}, f32[16,2304]{1,0:T(8,128)S(1)}, u32[]{:S(2)}, u32[]{:S(2)}) collective-permute-start(f32[16,2304]{1,0:T(8,128)S(1)} %get-tuple-element.1238), channel_id=1, source_target_pairs={{0,8},{8,16},{16,24},{24,0},{1,9},{9,17},{17,25},{25,1},{2,10},{10... | collective-permute-start | bytes 442376 | tf_op jit(solution)/shard_map/ppermute | solution.py:282
  134.7 9.2 %collective-permute-start.38 = (f32[16,2304]{1,0:T(8,128)S(1)}, f32[16,2304]{1,0:T(8,128)S(1)}, u32[]{:S(2)}, u32[]{:S(2)}) collective-permute-start(f32[16,2304]{1,0:T(8,128)S(1)} %collective-permute-done.36), channel_id=1, source_target_pairs={{0,8},{8,16},{16,24},{24,0},{1,9},{9,17},{17,25},{25,1},{2,10},{10... | collective-permute-start | bytes 442376 | tf_op jit(solution)/shard_map/ppermute | solution.py:282
  145.7 21.4 %collective-permute-start.42 = (f32[64,2304]{1,0:T(8,128)S(1)}, f32[64,2304]{1,0:T(8,128)S(1)}, u32[]{:S(2)}, u32[]{:S(2)}) collective-permute-start(f32[64,2304]{1,0:T(8,128)S(1)} %pad_maximum_fusion.12.first.refs_0_), channel_id=1, source_target_pairs={{0,4},{4,0},{1,5},{5,1},{2,6},{6,2},{3,7},{7,3},{8,12},{12,8},{9,1... | collective-permute-start | bytes 1769480 | tf_op jit(solution)/shard_map/ppermute | solution.py:269
  158.0 12.4 %collective-permute-start.50 = (f32[16,2304]{1,0:T(8,128)S(1)}, f32[16,2304]{1,0:T(8,128)S(1)}, u32[]{:S(2)}, u32[]{:S(2)}) collective-permute-start(f32[16,2304]{1,0:T(8,128)S(1)} %add_subtract_fusion.2), channel_id=1, source_target_pairs={{0,8},{8,16},{16,24},{24,0},{1,9},{9,17},{17,25},{25,1},{2,10},{10... | collective-permute-start | bytes 442376 | tf_op jit(solution)/shard_map/ppermute | solution.py:282
  165.1 9.4 %collective-permute-start.51 = (f32[16,2304]{1,0:T(8,128)S(1)}, f32[16,2304]{1,0:T(8,128)S(1)}, u32[]{:S(2)}, u32[]{:S(2)}) collective-permute-start(f32[16,2304]{1,0:T(8,128)S(1)} %add_subtract_fusion.2), channel_id=1, source_target_pairs={{0,24},{8,0},{16,8},{24,16},{1,25},{9,1},{17,9},{25,17},{2,26},{10... | collective-permute-start | bytes 442376 | tf_op jit(solution)/shard_map/ppermute | solution.py:282
  165.2 10.5 %collective-permute-start.54 = (f32[16,2304]{1,0:T(8,128)S(1)}, f32[16,2304]{1,0:T(8,128)S(1)}, u32[]{:S(2)}, u32[]{:S(2)}) collective-permute-start(f32[16,2304]{1,0:T(8,128)S(1)} %add_subtract_fusion.1), channel_id=1, source_target_pairs={{0,8},{8,16},{16,24},{24,0},{1,9},{9,17},{17,25},{25,1},{2,10},{10... | collective-permute-start | bytes 442376 | tf_op jit(solution)/shard_map/ppermute | solution.py:282
  172.3 11.0 %collective-permute-start.57 = (f32[128,1024]{1,0:T(8,128)S(1)}, f32[128,1024]{1,0:T(8,128)S(1)}, u32[]{:S(2)}, u32[]{:S(2)}) collective-permute-start(f32[128,1024]{1,0:T(8,128)S(1)} %get-tuple-element.1405), channel_id=1, source_target_pairs={{0,1},{1,0},{2,3},{3,2},{4,5},{5,4},{6,7},{7,6},{8,9},{9,8},{10,11... | collective-permute-start | bytes 1572872 | tf_op jit(solution)/shard_map/ppermute | solution.py:269
  175.7 9.1 %collective-permute-start.56 = (f32[16,2304]{1,0:T(8,128)S(1)}, f32[16,2304]{1,0:T(8,128)S(1)}, u32[]{:S(2)}, u32[]{:S(2)}) collective-permute-start(f32[16,2304]{1,0:T(8,128)S(1)} %add.161), channel_id=1, source_target_pairs={{0,24},{8,0},{16,8},{24,16},{1,25},{9,1},{17,9},{25,17},{2,26},{10... | collective-permute-start | bytes 442376 | tf_op jit(solution)/shard_map/ppermute | solution.py:282
  181.7 15.7 %collective-permute-start.55 = (f32[64,2304]{1,0:T(8,128)S(1)}, f32[64,2304]{1,0:T(8,128)S(1)}, u32[]{:S(2)}, u32[]{:S(2)}) collective-permute-start(f32[64,2304]{1,0:T(8,128)S(1)} %pad_maximum_fusion.13.first.refs_2_), channel_id=1, source_target_pairs={{0,4},{4,0},{1,5},{5,1},{2,6},{6,2},{3,7},{7,3},{8,12},{12,8},{9,1... | collective-permute-start | bytes 1769480 | tf_op jit(solution)/shard_map/ppermute | solution.py:269
  195.7 22.8 %collective-permute-start.65 = (f32[128,2304]{1,0:T(8,128)S(1)}, f32[128,2304]{1,0:T(8,128)S(1)}, u32[]{:S(2)}, u32[]{:S(2)}) collective-permute-start(f32[128,2304]{1,0:T(8,128)S(1)} %pad_maximum_fusion.4), channel_id=1, source_target_pairs={{0,2},{2,0},{1,3},{3,1},{4,6},{6,4},{5,7},{7,5},{8,10},{10,8},{9,1... | collective-permute-start | bytes 3538952 | tf_op jit(solution)/shard_map/ppermute | solution.py:269
  195.7 16.1 %collective-permute-start.61 = (f32[64,2304]{1,0:T(8,128)S(1)}, f32[64,2304]{1,0:T(8,128)S(1)}, u32[]{:S(2)}, u32[]{:S(2)}) collective-permute-start(f32[64,2304]{1,0:T(8,128)S(1)} %pad_maximum_fusion.14.first.refs_4_), channel_id=1, source_target_pairs={{0,4},{4,0},{1,5},{5,1},{2,6},{6,2},{3,7},{7,3},{8,12},{12,8},{9,1... | collective-permute-start | bytes 1769480 | tf_op jit(solution)/shard_map/ppermute | solution.py:269
  197.2 31.2 %collective-permute-start.67 = (f32[128,512]{1,0:T(8,128)S(1)}, f32[128,512]{1,0:T(8,128)S(1)}, u32[]{:S(2)}, u32[]{:S(2)}) collective-permute-start(f32[128,512]{1,0:T(8,128)S(1)} %get-tuple-element.1520), channel_id=1, source_target_pairs={{0,2},{2,0},{1,3},{3,1},{4,6},{6,4},{5,7},{7,5},{8,10},{10,8},{9,1... | collective-permute-start | bytes 786440 | tf_op jit(solution)/shard_map/ppermute | solution.py:269
  200.6 14.4 %collective-permute-start.63 = (f32[128,1024]{1,0:T(8,128)S(1)}, f32[128,1024]{1,0:T(8,128)S(1)}, u32[]{:S(2)}, u32[]{:S(2)}) collective-permute-start(f32[128,1024]{1,0:T(8,128)S(1)} %get-tuple-element.1481), channel_id=1, source_target_pairs={{0,1},{1,0},{2,3},{3,2},{4,5},{5,4},{6,7},{7,6},{8,9},{9,8},{10,11... | collective-permute-start | bytes 1572872 | tf_op jit(solution)/shard_map/ppermute | solution.py:269
  202.8 21.3 %collective-permute-start.64 = (f32[64,2304]{1,0:T(8,128)S(1)}, f32[64,2304]{1,0:T(8,128)S(1)}, u32[]{:S(2)}, u32[]{:S(2)}) collective-permute-start(f32[64,2304]{1,0:T(8,128)S(1)} %pad_maximum_fusion.15.first.refs_6_), channel_id=1, source_target_pairs={{0,4},{4,0},{1,5},{5,1},{2,6},{6,2},{3,7},{7,3},{8,12},{12,8},{9,1... | collective-permute-start | bytes 1769480 | tf_op jit(solution)/shard_map/ppermute | solution.py:269
  211.8 20.9 %collective-permute-start.68 = (f32[128,2304]{1,0:T(8,128)S(1)}, f32[128,2304]{1,0:T(8,128)S(1)}, u32[]{:S(2)}, u32[]{:S(2)}) collective-permute-start(f32[128,2304]{1,0:T(8,128)S(1)} %pad_maximum_fusion.5), channel_id=1, source_target_pairs={{0,2},{2,0},{1,3},{3,1},{4,6},{6,4},{5,7},{7,5},{8,10},{10,8},{9,1... | collective-permute-start | bytes 3538952 | tf_op jit(solution)/shard_map/ppermute | solution.py:269
  216.0 14.3 %collective-permute-start.66 = (f32[128,1024]{1,0:T(8,128)S(1)}, f32[128,1024]{1,0:T(8,128)S(1)}, u32[]{:S(2)}, u32[]{:S(2)}) collective-permute-start(f32[128,1024]{1,0:T(8,128)S(1)} %get-tuple-element.1526), channel_id=1, source_target_pairs={{0,1},{1,0},{2,3},{3,2},{4,5},{5,4},{6,7},{7,6},{8,9},{9,8},{10,11... | collective-permute-start | bytes 1572872 | tf_op jit(solution)/shard_map/ppermute | solution.py:269
  218.5 15.4 %collective-permute-start.69 = (f32[128,512]{1,0:T(8,128)}, f32[128,512]{1,0:T(8,128)S(1)}, u32[]{:S(2)}, u32[]{:S(2)}) collective-permute-start(f32[128,512]{1,0:T(8,128)} %get-tuple-element.1544), channel_id=1, source_target_pairs={{0,2},{2,0},{1,3},{3,1},{4,6},{6,4},{5,7},{7,5},{8,10},{10,8},{9,1... | collective-permute-start | bytes 786440 | tf_op jit(solution)/shard_map/ppermute | solution.py:269
  224.0 10.5 %collective-permute-start.71 = (f32[128,2304]{1,0:T(8,128)}, f32[128,2304]{1,0:T(8,128)}, u32[]{:S(2)}, u32[]{:S(2)}) collective-permute-start(f32[128,2304]{1,0:T(8,128)} %pad_maximum_fusion.6), channel_id=1, source_target_pairs={{0,2},{2,0},{1,3},{3,1},{4,6},{6,4},{5,7},{7,5},{8,10},{10,8},{9,1... | collective-permute-start | bytes 3538952 | tf_op jit(solution)/shard_map/ppermute | solution.py:269
  230.3 18.6 %collective-permute-start.74 = (f32[128,1024]{1,0:T(8,128)S(1)}, f32[128,1024]{1,0:T(8,128)S(1)}, u32[]{:S(2)}, u32[]{:S(2)}) collective-permute-start(f32[128,1024]{1,0:T(8,128)S(1)} %get-tuple-element.1601), channel_id=1, source_target_pairs={{0,1},{1,0},{2,3},{3,2},{4,5},{5,4},{6,7},{7,6},{8,9},{9,8},{10,11... | collective-permute-start | bytes 1572872 | tf_op jit(solution)/shard_map/ppermute | solution.py:269
  234.0 14.3 %collective-permute-start.70 = (f32[2,2304]{1,0:T(2,128)S(1)}, f32[2,2304]{1,0:T(2,128)S(1)}, u32[]{:S(2)}, u32[]{:S(2)}) collective-permute-start(f32[2,2304]{1,0:T(2,128)S(1)} %pad_maximum_fusion.16), channel_id=1, source_target_pairs={{0,2},{2,0},{1,3},{3,1},{4,6},{6,4},{5,7},{7,5},{8,10},{10,8},{9,1... | collective-permute-start | bytes 55304 | tf_op jit(solution)/shard_map/ppermute | solution.py:269
  234.0 15.8 %collective-permute-start.75 = (f32[128,512]{1,0:T(8,128)S(1)}, f32[128,512]{1,0:T(8,128)S(1)}, u32[]{:S(2)}, u32[]{:S(2)}) collective-permute-start(f32[128,512]{1,0:T(8,128)S(1)} %get-tuple-element.1595), channel_id=1, source_target_pairs={{0,2},{2,0},{1,3},{3,1},{4,6},{6,4},{5,7},{7,5},{8,10},{10,8},{9,1... | collective-permute-start | bytes 786440 | tf_op jit(solution)/shard_map/ppermute | solution.py:269
  249.9 14.5 %collective-permute-start.73 = (f32[1]{0:T(128)}, f32[1]{0:T(128)}, u32[]{:S(2)}, u32[]{:S(2)}) collective-permute-start(f32[1]{0:T(128)} %bitcast.6), channel_id=1, source_target_pairs={{0,1},{1,0},{2,3},{3,2},{4,5},{5,4},{6,7},{7,6},{8,9},{9,8},{10,11... | collective-permute-start | bytes 20 | tf_op jit(solution)/shard_map/ppermute | solution.py:269
  (56 other events, 434.4 us)
